TPU v7x, 512 devices: a whole 4x4x16 slice. The times are simulated.
512 devices in a mesh: row: 16 (over z_lo, core), col: 32 (over x, z_hi, y).
Axes of the slice: x: 4, y: 4, z: 16 (z_hi: 2, z_lo: 8; z = z_hi * 8 + z_lo), core: 2. Of those that a mesh axis runs over, the one named last changes fastest.
Arguments:
- pair: bfloat16 [256, 256, 128], P('row', 'col'), may hold values from -6 to 6
- pair_mask: int32 [256, 256], P('row', 'col'), may hold values 0 or 1
- contact_mask: int32 [256, 256], P('row', 'col'), may hold values 0 or 1
- dilations: int32 [2], replicated, may hold values from 1 to 8, as said below
- w_proj: bfloat16 [128, 512], replicated, may hold values from -0.5 to 0.5
- w_gate: bfloat16 [128, 128], replicated, may hold values from -0.5 to 0.5
- w_out: bfloat16 [128, 128], replicated, may hold values from -0.5 to 0.5
- conv_one: bfloat16 [9, 128, 128], replicated, may hold values from -0.1875 to 0.1875
- conv_two: bfloat16 [9, 128, 128], replicated, may hold values from -0.1875 to 0.1875
- cotangent: bfloat16 [256, 256, 128], P('row', 'col'), may hold values from -6 to 6
Outputs:
- output: bfloat16 [256, 256, 128], P('row', 'col')
- grad_pair: bfloat16 [256, 256, 128], P('row', 'col')
- grad_one: float32 [9, 128, 128], replicated
- grad_two: float32 [9, 128, 128], replicated
Inputs may be any that keep to these rules, and one draw needn't show every extreme that they name: `dilations`: one of the two rates equals 8, the other is smaller.
All inputs are finite; a program needn't handle non-finite values. No bound on the sum of `pair_mask` or of `contact_mask` on one device may be relied on, other than what follows from the above.
Results may differ from a plain program's by a relative error of at most 0.015.
Values may be sent and summed in bfloat16 or wider, within the bound.
A program may use at most 64 MiB of HBM per device.

v0:
```python
import jax
import jax.numpy as jnp
from jax import lax
from jax.sharding import PartitionSpec as P

DMAX = 8


EPSILON = 1e-05


def with_halo(block, sides, width):
    for axis, dim in sides:
        count = lax.axis_size(axis)
        forward = [(i, i + 1) for i in range(count - 1)]
        backward = [(target, source) for source, target in forward]
        low = lax.ppermute(
            lax.slice_in_dim(block, block.shape[dim] - width, None, axis=dim), axis, forward
        )
        high = lax.ppermute(lax.slice_in_dim(block, 0, width, axis=dim), axis, backward)
        block = jnp.concatenate([low, block, high], axis=dim)
    return block


def broadcast(x, axis, root):
    mine = lax.axis_index(axis) == root
    return lax.psum(jnp.where(mine, x, jnp.zeros_like(x)), axis)


def layer_norm(values):
    centre = values - jnp.mean(values, axis=-1, keepdims=True)
    spread = jnp.mean(centre * centre, axis=-1, keepdims=True)
    return centre * lax.rsqrt(spread + EPSILON)


def with_rim(field):
    return with_halo(field, (("row", 0), ("col", 1)), DMAX)


def gather_taps(padded, dilation, mirrored, height, breadth):
    windows = []
    for tap_index in range(9):
        row_tap = tap_index // 3
        col_tap = tap_index % 3
        if mirrored:
            row_tap = 2 - row_tap
            col_tap = 2 - col_tap
        row_start = DMAX + (row_tap - 1) * dilation
        col_start = DMAX + (col_tap - 1) * dilation
        windows.append(
            lax.dynamic_slice(
                padded, (row_start, col_start, jnp.int32(0)), (height, breadth, padded.shape[2])
            )
        )
    return jnp.concatenate(windows, axis=2).reshape(height * breadth, -1)


def local(
    pair, pair_mask, contact_mask, dilations, w_proj, w_gate, w_out, conv_one, conv_two, cotangent
):
    height, breadth, channels = pair.shape
    hidden = w_out.shape[0]
    row_count = lax.axis_size("row")
    col_count = lax.axis_size("col")
    ratio = col_count // row_count
    row_place = lax.axis_index("row")
    col_place = lax.axis_index("col")
    tokens = breadth * col_count
    pixels = height * breadth
    pair_flat = pair.astype(jnp.float32).reshape(pixels, channels)
    normed = layer_norm(pair_flat).astype(jnp.bfloat16)
    projected = jnp.dot(normed, w_proj, preferred_element_type=jnp.float32)
    mask_col = pair_mask.reshape(pixels, 1).astype(jnp.float32)
    left_side = (
        (mask_col * jax.nn.sigmoid(projected[:, hidden : 2 * hidden]) * projected[:, :hidden])
        .astype(jnp.bfloat16)
        .reshape(height, breadth, hidden)
    )
    right_side = (
        (
            mask_col
            * jax.nn.sigmoid(projected[:, 3 * hidden :])
            * projected[:, 2 * hidden : 3 * hidden]
        )
        .astype(jnp.bfloat16)
        .reshape(height, breadth, hidden)
    )
    right_all = lax.all_gather(right_side, "col", axis=1, tiled=True)
    offset = jnp.clip(col_place * breadth - row_place * height, 0, height - breadth)
    right_local = lax.dynamic_slice_in_dim(right_all, offset, breadth, 0)
    right_rows = broadcast(right_local, "row", col_place // ratio)
    products = jnp.einsum(
        "ikh,jkh->ijh",
        lax.all_gather(left_side, "col", axis=1, tiled=True),
        right_rows,
        preferred_element_type=jnp.float32,
    )
    product_norm = layer_norm(products.reshape(pixels, hidden)).astype(jnp.bfloat16)
    gating = jax.nn.sigmoid(jnp.dot(normed, w_gate, preferred_element_type=jnp.float32))
    updated = (
        pair_flat + gating * jnp.dot(product_norm, w_out, preferred_element_type=jnp.float32)
    ).astype(jnp.bfloat16)
    updated_f = updated.astype(jnp.float32)
    centre = updated_f - jnp.mean(updated_f, axis=-1, keepdims=True)
    inv_spread = lax.rsqrt(jnp.mean(centre * centre, axis=-1, keepdims=True) + EPSILON)
    scaled = centre * inv_spread
    contact = contact_mask.reshape(pixels, 1).astype(jnp.float32)
    first_in = (scaled * contact).astype(jnp.bfloat16).reshape(height, breadth, channels)
    rate_one = dilations[0]
    rate_two = dilations[1]
    first_taps = gather_taps(with_rim(first_in), rate_one, False, height, breadth)
    first_pre = jnp.dot(
        first_taps, conv_one.reshape(9 * channels, channels), preferred_element_type=jnp.float32
    )
    sigma = jax.nn.sigmoid(first_pre)
    second_in = (first_pre * sigma).astype(jnp.bfloat16).reshape(height, breadth, channels)
    second_taps = gather_taps(with_rim(second_in), rate_two, False, height, breadth)
    second_pre = jnp.dot(
        second_taps, conv_two.reshape(9 * channels, channels), preferred_element_type=jnp.float32
    )
    output = (updated_f + second_pre).astype(jnp.bfloat16).reshape(height, breadth, channels)
    cot_flat = cotangent.reshape(pixels, channels)
    grad_two = (
        lax.dot_general(
            second_taps, cot_flat, (((0,), (0,)), ((), ())), preferred_element_type=jnp.float32
        ).reshape(9, channels, channels)
        / tokens
    )
    cot_taps = gather_taps(with_rim(cotangent), rate_two, True, height, breadth)
    grad_hidden = jnp.dot(
        cot_taps,
        conv_two.transpose(0, 2, 1).reshape(9 * channels, channels),
        preferred_element_type=jnp.float32,
    )
    grad_pre = (grad_hidden * sigma * (1.0 + first_pre * (1.0 - sigma))).astype(jnp.bfloat16)
    grad_one = (
        lax.dot_general(
            first_taps, grad_pre, (((0,), (0,)), ((), ())), preferred_element_type=jnp.float32
        ).reshape(9, channels, channels)
        / tokens
    )
    grad_taps = gather_taps(
        with_rim(grad_pre.reshape(height, breadth, channels)), rate_one, True, height, breadth
    )
    grad_input = (
        jnp.dot(
            grad_taps,
            conv_one.transpose(0, 2, 1).reshape(9 * channels, channels),
            preferred_element_type=jnp.float32,
        )
        * contact
    )
    grad_norm = inv_spread * (
        grad_input
        - jnp.mean(grad_input, axis=-1, keepdims=True)
        - scaled * jnp.mean(grad_input * scaled, axis=-1, keepdims=True)
    )
    grad_pair = (
        (cot_flat.astype(jnp.float32) + grad_norm)
        .astype(jnp.bfloat16)
        .reshape(height, breadth, channels)
    )
    grad_one, grad_two = lax.psum((grad_one, grad_two), ("row", "col"))
    return (output, grad_pair, grad_one, grad_two)


def solution(mesh):
    in_specs = (
        P("row", "col", None),
        P("row", "col"),
        P("row", "col"),
        P(),
        P(),
        P(),
        P(),
        P(),
        P(),
        P("row", "col", None),
    )
    out_specs = (P("row", "col", None), P("row", "col", None), P(), P())
    return jax.shard_map(local, mesh=mesh, in_specs=in_specs, out_specs=out_specs, check_vma=False)
```

profile of v0, /device:TPU:1, one launch (start us, length us, event | category | flops | bytes accessed | tf_op | source)
XLA Modules:
  0.0 1222.8 jit_solution(12627889866462450348)
XLA Ops:
  7.2 0.9 convert_reduce_fusion
  8.1 0.9 fusion.15
  9.1 0.1 rsqrt.31
  9.2 0.7 convert_element_type.63
  10.1 1.0 fusion.36
  11.1 0.1 fusion.35
  11.2 0.6 copy.47
  11.9 0.9 copy.49
  12.8 0.7 fusion.40
  13.6 4.9 collective-permute-start.8
  18.5 5.1 collective-permute-start.9
  23.7 1.0 fusion.3
  24.7 0.8 constant_dynamic-update-slice_fusion.19
  25.5 1.3 collective-permute-start.11
  26.8 4.0 collective-permute-start.10
  30.8 1.3 fusion.41
  37.3 0.7 convert_element_type.70
  38.2 1.2 copy.55
  39.4 1.2 copy.56
  40.8 88.2 %all-gather.3.cloned.1.call-done = bf16[16,256,128]{2,0,1:T(8,128)(2,1)} async-done(((bf16[16,8,128]{2,0,1:T(8,128)(2,1)}), bf16[16,256,128]{2,0,1:T(8,128)(2,1)}) %all-gather.3.cloned.1.call-update) | async-done | bytes 1048592 | tf_op jit(solution)/shard_map/all_gather | solution.py:88
  129.0 1.4 constant_dynamic-slice_fusion
  130.3 0.6 copy.59
  130.9 0.8 broadcast_select_fusion
  131.9 0.8 constant_dynamic-update-slice_fusion.25
  132.8 309.2 %all-gather.5.cloned.1.call-done = bf16[16,256,128]{0,1,2:T(8,128)(2,1)} async-done(((bf16[16,8,128]{0,1,2:T(8,128)(2,1)}), bf16[16,256,128]{0,1,2:T(8,128)(2,1)}) %all-gather.5.cloned.1.call-update) | async-done | bytes 1048592 | tf_op jit(solution)/shard_map/all_gather | solution.py:94
  441.9 214.8 %all-reduce.4.cloned.1.call-done = bf16[8,256,128]{1,0,2:T(8,128)(2,1)} async-done(((bf16[8,256,128]{1,0,2:T(8,128)(2,1)}), bf16[8,256,128]{1,0,2:T(8,128)(2,1)}) %all-reduce.4.cloned.1.call-update) | async-done | bytes 524304 | tf_op jit(solution)/shard_map/psum | solution.py:27
  656.7 4.8 fusion.42
  661.6 0.1 div.64
  661.7 0.2 copy.50
  661.9 0.2 multiply_reduce_fusion
  662.2 0.1 rsqrt.33
  662.3 0.3 fusion.43
  662.6 0.2 multiply_reduce_fusion.2
  662.8 0.1 multiply_convert_fusion.1
  662.9 2.7 collective-permute-start.1
  665.6 2.9 collective-permute-start
  668.5 0.1 fusion.58
  668.6 0.7 collective-permute-done
  669.4 1.3 collective-permute-start.3
  670.7 4.0 collective-permute-start.2
  674.7 0.5 collective-permute-done.3
  675.3 1.1 collective-permute-done.2
  676.5 0.1 constant_dynamic-update-slice_fusion.4
  676.8 0.2 multiply_convert_fusion
  677.1 2.5 collective-permute-start.5
  679.6 4.4 collective-permute-start.4
  684.0 0.2 fusion.6
  684.2 1.9 collective-permute-start.13
  686.2 3.6 collective-permute-start.12
  689.8 0.2 copy.57
  690.0 1.0 convolution_multiply_fusion.1
  691.1 1.3 collective-permute-start.7
  692.4 4.6 collective-permute-start.6
  697.1 1.3 collective-permute-start.15
  698.4 4.0 collective-permute-start.14
  702.7 1.3 collective-permute-done.14
  704.4 0.2 copy.58
  704.6 1.0 convolution_multiply_fusion
  705.6 0.3 fusion.39
  706.0 0.8 fusion.9
  706.9 0.8 fusion.28
  707.6 504.9 %all-reduce.6.cloned.1.call-done = (f32[9,128,128]{2,1,0:T(8,128)}, f32[9,128,128]{2,1,0:T(8,128)}) async-done(((f32[9,128,128]{2,1,0:T(8,128)}, f32[9,128,128]{2,1,0:T(8,128)}), (f32[9,128,128]{2,1,0:T(8,128)}, f32[9,128,128]{2,1,0:T(8,128)})) %all-reduce.6.cloned.1.call-update) | async-done | bytes 1179664 | tf_op jit(solution)/shard_map/psum | solution.py:163
  1212.5 1.9 copy.97
  1214.4 1.9 copy.98
  (93 shorter events, 2.2 us)
Async XLA Ops:
  7.2 2.9 copy-start
  7.2 121.8 %all-gather.3.cloned.1.call-start = ((), (), s32[]{:S(2)}) async-start(), calls=%async_computation | async-start | bytes 1081344 | tf_op jit(solution)/shard_map/all_gather | solution.py:88
  11.8 430.1 %all-gather.5.cloned.1.call-start = ((), (), s32[]{:S(2)}) async-start(), calls=%async_computation.2 | async-start | bytes 8650752 | tf_op jit(solution)/shard_map/all_gather | solution.py:94
  12.8 643.9 %all-reduce.4.cloned.1.call-start = ((), (), s32[]{:S(2)}) async-start(), calls=%async_computation.1 | async-start | bytes 1048576 | tf_op jit(solution)/shard_map/psum | solution.py:27
  13.6 11.1 collective-permute-start.8
  18.5 7.0 collective-permute-start.9
  24.7 637.6 %copy-start.3 = (bf16[16,8,128]{2,1,0:T(8,128)(2,1)S(1)}, bf16[16,8,128]{2,1,0:T(8,128)(2,1)}, u32[]{:S(2)}) copy-start(bf16[16,8,128]{2,1,0:T(8,128)(2,1)} %param.10) | copy-start | bytes 98308
  24.7 637.6 %copy-start.5 = (bf16[128,128]{1,0:T(8,128)(2,1)S(1)}, bf16[128,128]{1,0:T(8,128)(2,1)}, u32[]{:S(2)}) copy-start(bf16[128,128]{1,0:T(8,128)(2,1)} %param.16) | copy-start | bytes 98308
  25.5 15.1 %collective-permute-start.11 = (bf16[32,8,128]{2,1,0:T(8,128)(2,1)S(1)}, bf16[32,8,128]{2,1,0:T(8,128)(2,1)S(1)}, u32[]{:S(2)}, u32[]{:S(2)}) collective-permute-start(bf16[32,8,128]{2,1,0:T(8,128)(2,1)S(1)} %constant_dynamic-update-slice_fusion.18), channel_id=1, source_target_pairs={{1,0},{2,1},{3,2},{4,3},{5,4},{6,5},{7,6},{8,7},{9,8},{10,9},{11,1... | collective-permute-start | bytes 196616 | tf_op jit(solution)/shard_map/ppermute | solution.py:20
  26.8 13.8 %collective-permute-start.10 = (bf16[32,8,128]{2,1,0:T(8,128)(2,1)S(1)}, bf16[32,8,128]{2,1,0:T(8,128)(2,1)S(1)}, u32[]{:S(2)}, u32[]{:S(2)}) collective-permute-start(bf16[32,8,128]{2,1,0:T(8,128)(2,1)S(1)} %constant_dynamic-update-slice_fusion.18), channel_id=1, source_target_pairs={{0,1},{1,2},{2,3},{3,4},{4,5},{5,6},{6,7},{7,8},{8,9},{9,10},{10,1... | collective-permute-start | bytes 196616 | tf_op jit(solution)/shard_map/ppermute | solution.py:17
  40.7 636.1 %copy-start.4 = (bf16[9,128,128]{2,1,0:T(8,128)(2,1)S(1)}, bf16[9,128,128]{2,1,0:T(8,128)(2,1)}, u32[]{:S(2)}) copy-start(bf16[9,128,128]{2,1,0:T(8,128)(2,1)} %param.17) | copy-start | bytes 884740
  131.8 1080.7 %all-reduce.6.cloned.1.call-start = ((), (), s32[]{:S(2)}) async-start(), calls=%async_computation.3 | async-start | bytes 2359296 | tf_op jit(solution)/shard_map/psum | solution.py:163
  132.7 571.9 %copy-start.2 = (bf16[16,8,128]{2,1,0:T(8,128)(2,1)S(1)}, bf16[16,8,128]{2,1,0:T(8,128)(2,1)}, u32[]{:S(2)}) copy-start(bf16[16,8,128]{2,1,0:T(8,128)(2,1)} %param.19) | copy-start | bytes 98308
  132.8 573.3 %copy-start.1 = (bf16[9,128,128]{2,1,0:T(8,128)(2,1)S(1)}, bf16[9,128,128]{2,1,0:T(8,128)(2,1)}, u32[]{:S(2)}) copy-start(bf16[9,128,128]{2,1,0:T(8,128)(2,1)} %param.18) | copy-start | bytes 884740
  662.9 5.7 collective-permute-start.1
  665.6 3.8 collective-permute-start
  669.4 5.9 collective-permute-start.3
  670.7 5.7 collective-permute-start.2
  677.1 14.0 %collective-permute-start.5 = (bf16[8,8,128]{2,1,0:T(8,128)(2,1)S(1)}, bf16[8,8,128]{2,1,0:T(8,128)(2,1)S(1)}, u32[]{:S(2)}, u32[]{:S(2)}) collective-permute-start(bf16[8,8,128]{2,1,0:T(8,128)(2,1)S(1)} %get-tuple-element.15), channel_id=1, source_target_pairs={{32,0},{64,32},{96,64},{128,96},{160,128},{192,160},{224,192},{256... | collective-permute-start | bytes 49160 | tf_op jit(solution)/shard_map/ppermute | solution.py:20
  679.6 11.5 collective-permute-start.4
  684.2 12.8 %collective-permute-start.13 = (bf16[8,8,128]{2,1,0:T(8,128)(2,1)S(1)}, bf16[8,8,128]{2,1,0:T(8,128)(2,1)S(1)}, u32[]{:S(2)}, u32[]{:S(2)}) collective-permute-start(bf16[8,8,128]{2,1,0:T(8,128)(2,1)S(1)} %get-tuple-element.11), channel_id=1, source_target_pairs={{32,0},{64,32},{96,64},{128,96},{160,128},{192,160},{224,192},{256... | collective-permute-start | bytes 49160 | tf_op jit(solution)/shard_map/ppermute | solution.py:20
  686.2 10.9 collective-permute-start.12
  691.1 11.3 collective-permute-start.7
  692.4 10.0 collective-permute-start.6
  697.1 5.7 collective-permute-start.15
  698.4 5.7 collective-permute-start.14
Sparse Core Ops, SparseCore 0:
  12.9 116.0 all-gather.2
  133.6 308.2 all-gather.4
  445.4 211.2 all-reduce.3
  706.1 506.3 all-reduce.5
where the time goes:
time: 1220 us
  waiting for transfers between devices  1120 us (92%)
  starting transfers between devices  50 us (4%)
  between operations  19.7 us (2%)
  local copies, waits for them, and re-layouts  15.9 us (1%)
    psum x1, waiting for transfers between devices, local(): grad_one, grad_two = lax.psum((grad_one, grad_two), ('row', 'col'))  505 us
    all_gather x1, waiting for transfers between devices, local(): lax.all_gather(left_side, 'col', axis=1, tiled=True)  309 us
    psum x1, waiting for transfers between devices, broadcast(): return lax.psum(jnp.where(mine, x, jnp.zeros_like(x)), axis)  215 us
    all_gather x1, waiting for transfers between devices, local(): right_all = lax.all_gather(right_side, 'col', axis=1, tiled=True)  88.2 us
    ppermute x8, starting transfers between devices, with_halo(): lax.ppermute(lax.slice_in_dim(block, block.shape[dim] - width, None, axis...  32.4 us
  transfers between devices with their start and end apart: 20, of which 8 were waited for; matrix products, arithmetic and copies ran while one was open for 1% of the time, Pallas kernels for 0%

commit v1 on v0

v1 whole, which is shorter than its diff:
```python
import functools

import jax
import jax.numpy as jnp
from jax import lax
from jax.experimental import pallas as pl
from jax.experimental.pallas import tpu as pltpu
from jax.sharding import PartitionSpec as P

EPSILON = 1e-05
MESH = pl.DeviceIdType.MESH
BF = jnp.bfloat16
F32 = jnp.float32
ROWS = 16
COLS = 32


def signal(sem, row, col):
    pl.semaphore_signal(sem, inc=1, device_id=(row, col), device_id_type=MESH)


def remote(src, dst, send_sem, recv_sem, row, col):
    return pltpu.make_async_remote_copy(
        src_ref=src,
        dst_ref=dst,
        send_sem=send_sem,
        recv_sem=recv_sem,
        device_id=(row, col),
        device_id_type=MESH,
    )


def wait_bytes(ref, sem):
    pltpu.make_async_copy(ref, ref, sem).wait()


def each(low, high, body):
    def step(k, carry):
        body(k)
        return carry

    lax.fori_loop(low, high, step, 0)


def plane_peer(col, k):
    x = lax.rem(col // 8 + k // 4, 4)
    y = lax.rem(lax.rem(col, 4) + lax.rem(k, 4), 4)
    return x * 8 + lax.rem(col // 4, 2) * 4 + y


def plane_slot(col):
    return (col // 8) * 4 + lax.rem(col, 4)


def layer_norm(values):
    centre = values - jnp.mean(values, axis=-1, keepdims=True)
    spread = jnp.mean(centre * centre, axis=-1, keepdims=True)
    return centre * lax.rsqrt(spread + EPSILON)


def mask_column(mask, height, breadth):
    pixels = height * breadth
    pix = lax.broadcasted_iota(jnp.int32, (pixels, height), 0) // breadth
    pick = (pix == lax.broadcasted_iota(jnp.int32, (pixels, height), 1)).astype(F32)
    spread = jnp.dot(pick, mask.astype(F32), preferred_element_type=F32)
    place = lax.rem(lax.broadcasted_iota(jnp.int32, (pixels, breadth), 0), breadth)
    lane = lax.broadcasted_iota(jnp.int32, (pixels, breadth), 1)
    return jnp.sum(jnp.where(place == lane, spread, 0.0), axis=1, keepdims=True)


def triangle_kernel(
    pair_ref, pmask_ref, cmask_ref, wproj_ref, wgate_ref, wout_ref, cot_ref,
    updated_ref, first_ref, cots_ref,
    left, right, halves, first, cots, sums,
    l_send, l_recv, l_far, r_send0, r_recv0, r_send, r_recv, r_relay,
    c_send, c_recv, c_send2, c_recv2, f_send, f_recv, f_send2, f_recv2,
):
    row = lax.axis_index("row")
    col = lax.axis_index("col")
    far = (col // 8) * 8 + (1 - lax.rem(col // 4, 2)) * 4 + lax.rem(col, 4)
    sibling = row + 1 - 2 * lax.rem(row, 2)
    turn_row = col // 2
    up = lax.rem(row + ROWS - 1, ROWS)
    down = lax.rem(row + 1, ROWS)
    barrier = pltpu.get_barrier_semaphore()
    each(1, 16, lambda k: signal(barrier, row, plane_peer(col, k)))
    each(1, 8, lambda k: signal(barrier, lax.rem(row + 2 * k, ROWS), col))
    signal(barrier, row, far)
    signal(barrier, sibling, col)
    for shift in (1, 2):
        signal(barrier, row, lax.rem(col + shift, COLS))
        signal(barrier, row, lax.rem(col + COLS - shift, COLS))
    signal(barrier, up, col)
    signal(barrier, down, col)
    for half in range(2):
        @pl.when((turn_row != row) | (2 * row + half != col))
        def _():
            signal(barrier, turn_row, 2 * row + half)

    pair = pair_ref[...].astype(F32)
    normed = layer_norm(pair).astype(BF)
    projected = jnp.dot(normed, wproj_ref[...], preferred_element_type=F32)
    mask = mask_column(pmask_ref[...], 16, 8)
    left[col] = (mask * jax.nn.sigmoid(projected[:, 128:256]) * projected[:, :128]).astype(BF)
    halves[...] = (
        (mask * jax.nn.sigmoid(projected[:, 384:]) * projected[:, 256:384])
        .astype(BF)
        .reshape(2, 64, 128)
    )
    cots[7] = cot_ref[...]

    diagonal = turn_row == row

    @pl.when(diagonal)
    def _():
        pl.semaphore_wait(barrier, 31)

    @pl.when(jnp.logical_not(diagonal))
    def _():
        pl.semaphore_wait(barrier, 32)

    for half in range(2):
        there = 2 * row + half

        @pl.when((turn_row != row) | (there != col))
        def _():
            remote(
                halves.at[half], right.at[col], r_send0.at[half],
                r_recv0.at[lax.rem(col, 2)], turn_row, there,
            ).start()

        @pl.when((turn_row == row) & (there == col))
        def _():
            right[col] = halves[half]

    mine = left.at[col]
    remote(mine, mine, l_send, l_far, row, far).start()
    each(1, 16, lambda k: remote(mine, mine, l_send, l_recv, row, plane_peer(col, k)).start())

    for half in range(2):
        there = 2 * row + half

        @pl.when((turn_row != row) | (there != col))
        def _():
            wait_bytes(halves.at[half], r_send0.at[half])
            wait_bytes(right.at[0], r_recv0.at[half])

    two = right.at[pl.ds(2 * row, 2)]
    each(1, 8, lambda k: remote(
        two, two, r_send, r_relay.at[row // 2], lax.rem(row + 2 * k, ROWS), col).start())
    remote(two, two, r_send, r_recv, sibling, col).start()

    far_block = left.at[far]
    wait_bytes(far_block, l_far)
    each(1, 16, lambda k: remote(
        far_block, far_block, l_send, l_recv, row, plane_peer(col, k)).start())

    def along_cols(buf, send_sem, recv_sem):
        for n, shift in enumerate((1, 2, -1, -2)):
            remote(
                buf.at[7], buf.at[7 - shift], send_sem.at[n], recv_sem.at[n],
                row, lax.rem(col + COLS + shift, COLS),
            ).start()

    def wait_cols(buf, send_sem, recv_sem):
        for n in range(4):
            wait_bytes(buf.at[7], send_sem.at[n])
            wait_bytes(buf.at[7], recv_sem.at[n])

    def along_rows(buf, send_sem, recv_sem):
        band = buf.at[pl.ds(5, 5)]
        remote(band, buf.at[pl.ds(0, 5)], send_sem.at[0], recv_sem.at[0], down, col).start()
        remote(band, buf.at[pl.ds(10, 5)], send_sem.at[1], recv_sem.at[1], up, col).start()

    def wait_rows(buf, send_sem, recv_sem):
        for n in range(2):
            wait_bytes(buf.at[pl.ds(5, 5)], send_sem.at[n])
            wait_bytes(buf.at[pl.ds(0, 5)], recv_sem.at[n])

    along_cols(cots, c_send, c_recv)

    def relay(k):
        p = lax.rem(row + ROWS - 2 * k, ROWS)
        block = right.at[pl.ds(2 * p, 2)]
        wait_bytes(block, r_relay.at[p // 2])
        remote(block, block, r_send, r_recv, sibling, col).start()

    each(1, 8, relay)
    gating = jax.nn.sigmoid(jnp.dot(normed, wgate_ref[...], preferred_element_type=F32))
    wait_cols(cots, c_send, c_recv)
    along_rows(cots, c_send2, c_recv2)

    wait_bytes(right.at[pl.ds(0, 16)], r_recv)
    wait_bytes(left.at[pl.ds(0, 30)], l_recv)

    for part in range(4):
        def add(c, total):
            a = left[c, pl.ds(part * 32, 32), :].astype(F32).reshape(4, 1, 8, 128)
            b = right[c].astype(F32).reshape(1, 8, 8, 128)
            return total + a * b

        total = lax.fori_loop(0, COLS, add, jnp.zeros((4, 8, 8, 128), F32))
        sums[pl.ds(part * 32, 32), :] = jnp.sum(total, axis=2).reshape(32, 128)

    product_norm = layer_norm(sums[...]).astype(BF)
    updated = (
        pair + gating * jnp.dot(product_norm, wout_ref[...], preferred_element_type=F32)
    ).astype(BF)
    updated_ref[...] = updated
    contact = mask_column(cmask_ref[...], 16, 8)
    first[7] = (layer_norm(updated.astype(F32)) * contact).astype(BF)
    along_cols(first, f_send, f_recv)
    wait_rows(cots, c_send2, c_recv2)
    cots_ref[...] = cots[...]
    wait_cols(first, f_send, f_recv)
    along_rows(first, f_send2, f_recv2)
    wait_bytes(right.at[pl.ds(0, 30)], r_send)
    wait_bytes(left.at[pl.ds(0, 31)], l_send)
    wait_rows(first, f_send2, f_recv2)
    first_ref[...] = first[...]


def conv_kernel(
    rates_ref, updated_ref, cmask_ref, first_ref, cots_ref, one_ref, two_ref,
    output_ref, gpair_ref, grads_ref,
    field, taps, cfield, ctaps, hidden, htaps, gpre, gtaps,
):
    row = lax.axis_index("row")
    col = lax.axis_index("col")
    one_rate = rates_ref[0]
    two_rate = rates_ref[1]

    to = lax.broadcasted_iota(jnp.int32, (128, 128), 0)
    at = lax.broadcasted_iota(jnp.int32, (128, 128), 1)
    flip = ((lax.rem(to, 16) * 8 + to // 16) == at).astype(BF)
    flip_back = ((lax.rem(to, 8) * 16 + to // 8) == at).astype(BF)

    def unfold(src, dst):
        for n in range(15):
            dr, dc = n // 5 - 1, n % 5 - 2
            inside = (row + dr >= 0) & (row + dr < ROWS) & (col + dc >= 0) & (col + dc < COLS)
            cell = jnp.dot(flip, src[n], preferred_element_type=F32)
            dst[pl.ds((dc + 2) * 8, 8), pl.ds((dr + 1) * 16, 16), :] = jnp.where(
                inside, cell, 0.0
            ).reshape(8, 16, 128)

    def shifted(src, dst, start, rate, length, sign):
        for r in range(3):
            wide = src.shape[1]
            move = lax.rem(2 * wide - (start + sign * (r - 1) * rate), wide)
            dst[r] = pltpu.roll(src[...], move, 1)[:, :length].astype(BF)

    def windows(src, start, rate, count, sign, rows=None):
        found = []
        for t in range(9):
            at = pl.ds(start + sign * (t % 3 - 1) * rate, count)
            piece = src[t // 3, at] if rows is None else src[t // 3, at, rows, :]
            found.append(piece.reshape(-1, 128))
        return jnp.concatenate(found, axis=1)

    unfold(first_ref, field)
    unfold(cots_ref, cfield)
    shifted(field, taps, 8, one_rate, 32, 1)
    shifted(cfield, ctaps, 8, two_rate, 32, -1)

    weights_one = one_ref[...].reshape(1152, 128)
    weights_two = two_ref[...].reshape(1152, 128)
    back_two = jnp.concatenate([two_ref[t].T for t in range(9)], axis=0)
    back_one = jnp.concatenate([one_ref[t].T for t in range(9)], axis=0)

    pre = jnp.dot(windows(taps, 8, one_rate, 24, 1), weights_one, preferred_element_type=F32)
    grad_hidden = jnp.dot(
        windows(ctaps, 8, two_rate, 24, -1), back_two, preferred_element_type=F32
    )
    c_at = lax.broadcasted_iota(jnp.int32, (24, 32, 128), 0) + (col * 8 - 8)
    r_at = lax.broadcasted_iota(jnp.int32, (24, 32, 128), 1) + (row * 16 - 8)
    inside = (c_at >= 0) & (c_at < 256) & (r_at >= 0) & (r_at < 256)
    sigma = jax.nn.sigmoid(pre)
    hidden[...] = jnp.where(inside, (pre * sigma).reshape(24, 32, 128), 0.0)
    gpre[...] = jnp.where(
        inside, (grad_hidden * sigma * (1.0 + pre * (1.0 - sigma))).reshape(24, 32, 128), 0.0
    )
    shifted(hidden, htaps, 8, two_rate, 16, 1)
    shifted(gpre, gtaps, 8, one_rate, 16, -1)
    cot_own = cfield[pl.ds(16, 8), pl.ds(16, 16), :].reshape(128, 128)
    gpre_own = gpre[pl.ds(8, 8), pl.ds(8, 16), :].reshape(128, 128).astype(BF)
    second_taps = windows(htaps, 8, two_rate, 8, 1)
    first_taps = windows(taps, 16, one_rate, 8, 1, pl.ds(8, 16))
    over = (((0,), (0,)), ((), ()))
    grads_ref[pl.ds(1152, 1152), :] = lax.dot_general(
        second_taps, cot_own.astype(BF), over, preferred_element_type=F32
    ).astype(BF)
    grads_ref[pl.ds(0, 1152), :] = lax.dot_general(
        first_taps, gpre_own, over, preferred_element_type=F32
    ).astype(BF)
    def back(value):
        return jnp.dot(flip_back, value, preferred_element_type=F32).astype(BF)

    second_pre = jnp.dot(back(second_taps), weights_two, preferred_element_type=F32)
    grad_in = jnp.dot(
        back(windows(gtaps, 8, one_rate, 8, -1)), back_one, preferred_element_type=F32
    )
    updated = updated_ref[...].astype(F32)
    output_ref[...] = (updated + second_pre).astype(BF)
    contact = mask_column(cmask_ref[...], 16, 8)
    grad_in = grad_in * contact
    centre = updated - jnp.mean(updated, axis=-1, keepdims=True)
    inv = lax.rsqrt(jnp.mean(centre * centre, axis=-1, keepdims=True) + EPSILON)
    scaled = centre * inv
    grad_norm = inv * (
        grad_in
        - jnp.mean(grad_in, axis=-1, keepdims=True)
        - scaled * jnp.mean(grad_in * scaled, axis=-1, keepdims=True)
    )
    gpair_ref[...] = (cots_ref[7].astype(F32) + grad_norm).astype(BF)


def reduce_kernel(
    grads_ref, out_ref, parts, own, pieces, final,
    send1, recv1, send2, recv2, send3, recv3, send4, recv4,
):
    row = lax.axis_index("row")
    col = lax.axis_index("col")
    me = plane_slot(col)
    place = row * 2 + lax.rem(col // 4, 2)
    base = (col // 8) * 8 + lax.rem(col, 4)

    def line(q):
        return q // 2, base + lax.rem(q, 2) * 4

    barrier = pltpu.get_barrier_semaphore()
    each(1, 16, lambda k: signal(barrier, row, plane_peer(col, k)))
    each(1, 32, lambda k: signal(barrier, *line(lax.rem(place + k, 32))))
    pl.semaphore_wait(barrier, 46)

    def scatter(k):
        peer = plane_peer(col, k)
        remote(grads_ref.at[plane_slot(peer)], parts.at[me], send1, recv1, row, peer).start()

    each(1, 16, scatter)
    parts[me] = grads_ref[me]
    most = parts.at[pl.ds(0, 15)]
    wait_bytes(most, recv1)
    total = parts[0].astype(F32)
    for n in range(1, 16):
        total = total + parts[n].astype(F32)
    own[...] = total.astype(BF).reshape(9, 16, 128)

    for j in range(9):
        @pl.when(place != 3 * j)
        def _():
            remote(own.at[j], pieces.at[place], send2, recv2, *line(3 * j)).start()

    owner = (lax.rem(place, 3) == 0) & (place < 27)
    piece = place // 3

    @pl.when(owner)
    def _():
        pieces[place] = own[piece]
        wait_bytes(own.at[pl.ds(0, 8)], send2)
        wait_bytes(pieces.at[pl.ds(0, 31)], recv2)
        total = pieces[0].astype(F32)
        for n in range(1, 32):
            total = total + pieces[n].astype(F32)
        final[me, piece] = total.astype(BF)
        block = final.at[me, piece]
        each(1, 32, lambda k: remote(
            block, block, send3, recv3, *line(lax.rem(place + k, 32))).start())
        wait_bytes(own.at[pl.ds(0, 8)], recv3)

    @pl.when(jnp.logical_not(owner))
    def _():
        wait_bytes(own, send2)
        wait_bytes(own, recv3)

    whole = final.at[me]
    each(1, 16, lambda k: remote(whole, whole, send4, recv4, row, plane_peer(col, k)).start())
    wait_bytes(most, send1)

    @pl.when(owner)
    def _():
        wait_bytes(pieces.at[pl.ds(0, 31)], send3)

    wait_bytes(final.at[pl.ds(0, 15)], recv4)
    wait_bytes(final.at[pl.ds(0, 15)], send4)
    out_ref[...] = final[...].reshape(16, 144, 128)


VMEM = pltpu.VMEM
DMA = pltpu.SemaphoreType.DMA


def whole(count):
    return [pl.BlockSpec(memory_space=pltpu.VMEM)] * count


def shape(dims, dtype):
    return jax.ShapeDtypeStruct(dims, dtype)


def local(
    pair, pair_mask, contact_mask, dilations, w_proj, w_gate, w_out, conv_one, conv_two, cotangent
):
    pair = pair.reshape(128, 128)
    cot = cotangent.reshape(128, 128)
    updated, first, cots = pl.pallas_call(
        triangle_kernel,
        out_shape=(shape((128, 128), BF), shape((15, 128, 128), BF), shape((15, 128, 128), BF)),
        in_specs=whole(7),
        out_specs=tuple(whole(3)),
        scratch_shapes=[
            VMEM((32, 128, 128), BF), VMEM((32, 64, 128), BF), VMEM((2, 64, 128), BF),
            VMEM((15, 128, 128), BF), VMEM((15, 128, 128), BF), VMEM((128, 128), F32),
            DMA, DMA, DMA, DMA((2,)), DMA((2,)), DMA, DMA, DMA((8,)),
            DMA((4,)), DMA((4,)), DMA((2,)), DMA((2,)),
            DMA((4,)), DMA((4,)), DMA((2,)), DMA((2,)),
        ],
        compiler_params=pltpu.CompilerParams(
            collective_id=1, has_side_effects=True, vmem_limit_bytes=40 << 20
        ),
    )(pair, pair_mask, contact_mask, w_proj, w_gate, w_out, cot)
    output, grad_pair, grads = pl.pallas_call(
        conv_kernel,
        out_shape=(shape((128, 128), BF), shape((128, 128), BF), shape((2304, 128), BF)),
        in_specs=[pl.BlockSpec(memory_space=pltpu.SMEM)] + whole(6),
        out_specs=tuple(whole(3)),
        scratch_shapes=[
            VMEM((40, 48, 128), F32), VMEM((3, 40, 32, 128), BF),
            VMEM((40, 48, 128), F32), VMEM((3, 40, 32, 128), BF),
            VMEM((24, 32, 128), F32), VMEM((3, 24, 16, 128), BF),
            VMEM((24, 32, 128), F32), VMEM((3, 24, 16, 128), BF),
        ],
        compiler_params=pltpu.CompilerParams(vmem_limit_bytes=40 << 20),
    )(dilations, updated, contact_mask, first, cots, conv_one, conv_two)
    total = pl.pallas_call(
        reduce_kernel,
        out_shape=shape((16, 144, 128), BF),
        in_specs=whole(1),
        out_specs=whole(1)[0],
        scratch_shapes=[
            VMEM((16, 144, 128), BF), VMEM((9, 16, 128), BF), VMEM((32, 16, 128), BF),
            VMEM((16, 9, 16, 128), BF), DMA, DMA, DMA, DMA, DMA, DMA, DMA, DMA,
        ],
        compiler_params=pltpu.CompilerParams(
            collective_id=2, has_side_effects=True, vmem_limit_bytes=40 << 20
        ),
    )(grads.reshape(16, 144, 128))
    total = total.reshape(2, 9, 128, 128).astype(F32) * (1.0 / 256.0)
    return (output.reshape(16, 8, 128), grad_pair.reshape(16, 8, 128), total[0], total[1])


def solution(mesh):
    in_specs = (
        P("row", "col", None), P("row", "col"), P("row", "col"), P(), P(), P(), P(), P(), P(),
        P("row", "col", None),
    )
    out_specs = (P("row", "col", None), P("row", "col", None), P(), P())
    return jax.shard_map(local, mesh=mesh, in_specs=in_specs, out_specs=out_specs, check_vma=False)
```

time: 1220 us -> 122 us (0.10)
  waiting for transfers between devices: 1120 us -> 0 us
  Pallas kernels: 0 us -> 112 us
  starting transfers between devices: 50 us -> 0 us
  between operations: 19.7 us -> 0.67 us
    psum x2 -> x0, waiting for transfers between devices: 720 us -> none  [the longest x1 505 us: local(): grad_one, grad_two = lax.psum((grad_one, grad_two), ('row', 'col'))]
    all_gather x2 -> x0, waiting for transfers between devices: 397 us -> none  [the longest x1 309 us: local(): lax.all_gather(left_side, 'col', axis=1, tiled=True)]
    pallas_call x0 -> x3, Pallas kernels: none -> 112 us  [the longest x1 60.2 us: local(): pl.pallas_call(triangle_kernel, out_shape=(shape((128, 128), BF), shape((...]
    ppermute x16 -> x0, starting transfers between devices: 49.8 us -> none  [the longest x8 32.4 us: with_halo(): lax.ppermute(lax.slice_in_dim(block, block.shape[dim] - width, None, axis...]
  transfers between devices with their start and end apart: 20 -> 0, of which waited for: 8 -> 0; matrix products, arithmetic and copies ran while one was open for 1% -> 0% of each run, Pallas kernels for 0% -> 0%
where the time goes in v1:
time: 122 us; the launch traced here: 121 us
  Pallas kernels  112 us (92%)
  local copies, waits for them, and re-layouts  9.11 us (7%)
    pallas_call x1, Pallas kernels, local(): pl.pallas_call(triangle_kernel, out_shape=(shape((128, 128), BF), shape((...  60.2 us
    pallas_call x1, Pallas kernels, local(): pl.pallas_call(reduce_kernel, out_shape=shape((16, 144, 128), BF), in_spe...  47.1 us
    unnamed x18, local copies, waits for them, and re-layouts  8.02 us
    pallas_call x1, Pallas kernels, local(): pl.pallas_call(conv_kernel, out_shape=(shape((128, 128), BF), shape((128,...  4.31 us

profile of v1, /device:TPU:1, one launch (start us, length us, event | category | flops | bytes accessed | tf_op | source)
XLA Modules:
  0.0 121.4 jit_solution(9430946676057825995)
XLA Ops:
  0.6 0.8 copy.15.cmask_ref
  1.4 0.8 copy.14.pmask_ref
  2.1 0.0 copy-start.2
  2.1 0.9 copy-done.2
  3.1 0.0 copy-start.3
  3.1 0.8 copy-done.3
  3.8 0.0 copy-start.4
  3.8 0.8 copy-done.4
  4.6 0.0 copy-start.5
  4.6 0.8 copy-done.5
  5.3 0.0 copy-start.6
  5.3 0.8 copy-done.6
  6.1 60.2 %shard_map.129 = (bf16[128,128]{1,0:T(8,128)(2,1)S(1)}, bf16[15,128,128]{2,1,0:T(8,128)(2,1)S(1)}, bf16[15,128,128]{2,1,0:T(8,128)(2,1)S(1)}) custom-call(bf16[128,128]{1,0:T(8,128)(2,1)S(1)} %bitcast.8, s32[16,8]{1,0:T(8,128)S(1)} %copy.14.pmask_ref, s32[16,8]{1,0:T(8,128)S(1)} %copy.15.cmask_ref, bf16[128,512]{1,0:T(8,128)(2,1)S(1)} %copy-done.2, ...), custom_call_target="tpu_custom_call" | custom-call | tf_op jit(solution)/shard_map/pallas_call | solution.py:406
  66.3 0.0 copy-start
  66.3 1.0 copy-done
  67.2 0.0 copy-start.1
  67.2 1.0 copy-done.1
  68.2 0.0 copy-start.7
  68.2 0.7 copy-done.7
  68.9 4.3 %shard_map.130 = (bf16[128,128]{1,0:T(8,128)(2,1)}, bf16[128,128]{1,0:T(8,128)(2,1)}, bf16[2304,128]{1,0:T(8,128)(2,1)S(1)}) custom-call(s32[2]{0:T(128)S(1)} %copy-done.7, bf16[128,128]{1,0:T(8,128)(2,1)S(1)} %get-tuple-element.10.updated_ref, s32[16,8]{1,0:T(8,128)S(1)} %copy.15.cmask_ref, bf16[15,128,128]{2,1,0:T(8,128)(2,1)S(1)} %get-tuple-element.11.first_ref, ...), custom_call_target="tpu_custom_call" | custom-call | tf_op jit(solution)/shard_map/pallas_call | solution.py:422
  73.2 47.1 %shard_map.131 = bf16[16,144,128]{2,1,0:T(8,128)(2,1)S(1)} custom-call(bf16[16,144,128]{2,1,0:T(8,128)(2,1)S(1)} %bitcast.7), custom_call_target="tpu_custom_call" | custom-call | tf_op jit(solution)/shard_map/pallas_call | solution.py:435
  120.2 0.1 convert_multiply_fusion
  120.3 1.1 fusion
Async XLA Ops:
  2.1 0.9 copy-start.2
  3.1 0.8 copy-start.3
  3.8 0.8 copy-start.4
  4.6 0.8 copy-start.5
  5.3 0.8 copy-start.6
  66.3 1.0 copy-start
  67.2 1.0 copy-start.1
  68.2 0.7 copy-start.7

commit v2 on v0

v2 whole, which is shorter than its diff:
```python
import jax
import jax.numpy as jnp
from jax import lax
from jax.experimental import pallas as pl
from jax.experimental.pallas import tpu as pltpu
from jax.sharding import PartitionSpec as P

EPSILON = 1e-05
MESH = pl.DeviceIdType.MESH
BF = jnp.bfloat16
F32 = jnp.float32
ROWS = 16
COLS = 32
SHIFTS = (1, 2, -1, -2)


def signal(sem, row, col):
    pl.semaphore_signal(sem, inc=1, device_id=(row, col), device_id_type=MESH)


def remote(src, dst, send_sem, recv_sem, row, col):
    return pltpu.make_async_remote_copy(
        src_ref=src,
        dst_ref=dst,
        send_sem=send_sem,
        recv_sem=recv_sem,
        device_id=(row, col),
        device_id_type=MESH,
    )


def wait_bytes(ref, sem):
    pltpu.make_async_copy(ref, ref, sem).wait()


def each(low, high, body):
    def step(k, carry):
        body(k)
        return carry

    lax.fori_loop(low, high, step, 0)


def plane_peer(col, k):
    x = lax.rem(col // 8 + k // 4, 4)
    y = lax.rem(lax.rem(col, 4) + lax.rem(k, 4), 4)
    return x * 8 + lax.rem(col // 4, 2) * 4 + y


def plane_slot(col):
    return (col // 8) * 4 + lax.rem(col, 4)


def on_map(col):
    return (col >= 0) & (col < COLS)


def layer_norm(values):
    centre = values - jnp.mean(values, axis=-1, keepdims=True)
    spread = jnp.mean(centre * centre, axis=-1, keepdims=True)
    return centre * lax.rsqrt(spread + EPSILON)


def mask_column(mask):
    pix = lax.broadcasted_iota(jnp.int32, (128, 8), 0)
    lane = lax.broadcasted_iota(jnp.int32, (128, 8), 1)
    pick = (lax.rem(pix, 8) == lane).astype(F32)
    spread = jnp.dot(pick, mask.astype(F32), preferred_element_type=F32)
    place = lax.broadcasted_iota(jnp.int32, (128, 16), 0) // 8
    at = lax.broadcasted_iota(jnp.int32, (128, 16), 1)
    return jnp.sum(jnp.where(place == at, spread, 0.0), axis=1, keepdims=True)


def shifted(src, dst, start, rate, length, sign):
    wide = src.shape[1]
    for r in range(3):
        move = lax.rem(2 * wide - (start + sign * (r - 1) * rate), wide)
        dst[r] = pltpu.roll(src[...], move, 1)[:, :length].astype(BF)


def windows(src, start, rate, count, sign, rows=None):
    found = []
    for t in range(9):
        at = pl.ds(start + sign * (t % 3 - 1) * rate, count)
        piece = src[t // 3, at] if rows is None else src[t // 3, at, rows, :]
        found.append(piece.reshape(-1, 128))
    return jnp.concatenate(found, axis=1)


def kernel(
    pair_h, pmask_h, cmask_h, rates_h, wproj_h, wgate_h, wout_h, one_h, two_h, cot_h,
    output_ref, gpair_ref, total_ref,
    pair_v, pmask_v, cmask_v, rates_s, wproj_v, wgate_v, wout_v, one_v, two_v, in_sem,
    left, right, halves, first, cots, sums,
    field, taps, cfield, ctaps, hidden, htaps, gpre, gtaps, ghid,
    grads, parts, own, pieces, final,
    l_send, l_recv, l_far, r_send0, r_recv0, r_send, r_recv, r_relay,
    c_send, c_recv, c_send2, c_recv2, f_send, f_recv, f_send2, f_recv2,
    send1, recv1, send2, recv2, send3, recv3, send4, recv4,
):
    row = lax.axis_index("row")
    col = lax.axis_index("col")
    far = (col // 8) * 8 + (1 - lax.rem(col // 4, 2)) * 4 + lax.rem(col, 4)
    sibling = row + 1 - 2 * lax.rem(row, 2)
    turn_row = col // 2
    turn_col = 4 * lax.rem(row, 8)
    me = plane_slot(col)
    place = row * 2 + lax.rem(col // 4, 2)
    base = (col // 8) * 8 + lax.rem(col, 4)

    def line(q):
        return q // 2, base + lax.rem(q, 2) * 4

    with jax.named_scope("start"):
        loads = [
            pltpu.make_async_copy(src, dst, in_sem.at[n])
            for n, (src, dst) in enumerate((
                (pair_h, pair_v), (pmask_h, pmask_v), (wproj_h, wproj_v), (cot_h, cots.at[7]),
                (wgate_h, wgate_v), (wout_h, wout_v), (cmask_h, cmask_v), (rates_h, rates_s),
                (two_h, two_v), (one_h, one_v),
            ))
        ]
        for load in loads:
            load.start()
        barrier = pltpu.get_barrier_semaphore()
        each(1, 16, lambda k: signal(barrier, row, plane_peer(col, k)))
        each(1, 32, lambda k: signal(barrier, *line(lax.rem(place + k, 32))))
        for shift in (1, 2, -1, -2):
            @pl.when(on_map(col + shift))
            def _():
                signal(barrier, row, col + shift)
        for n in range(4):
            @pl.when((turn_row != row) | (turn_col + n != col))
            def _():
                signal(barrier, turn_row, turn_col + n)

    with jax.named_scope("project"):
        for n in (0, 1, 2):
            loads[n].wait()
        pair = pair_v[...].astype(F32)
        normed = layer_norm(pair).astype(BF)
        projected = jnp.dot(normed, wproj_v[...], preferred_element_type=F32)
        mask = mask_column(pmask_v[...])
        left[col] = (mask * jax.nn.sigmoid(projected[:, 128:256]) * projected[:, :128]).astype(BF)
        halves[...] = (
            (mask * jax.nn.sigmoid(projected[:, 384:]) * projected[:, 256:384])
            .astype(BF)
            .reshape(2, 64, 128)
        )
        loads[3].wait()

    with jax.named_scope("barrier"):
        fixed = (turn_row == row) & (lax.rem(row, 8) == col // 4)
        pl.semaphore_wait(
            barrier,
            50 - jnp.where(fixed, 1, 0) + jnp.minimum(col, 2) + jnp.minimum(COLS - 1 - col, 2),
        )

    with jax.named_scope("turn"):
        def turn(half, low):
            return low * 8 + col // 4, 2 * row + half

        for half in range(2):
            for low in range(2):
                t_row, t_col = turn(half, low)

                @pl.when((t_row != row) | (t_col != col))
                def _():
                    remote(
                        halves.at[half], right.at[col], r_send0.at[2 * half + low],
                        r_recv0.at[lax.rem(col, 4)], t_row, t_col,
                    ).start()

                @pl.when((t_row == row) & (t_col == col))
                def _():
                    right[col] = halves[half]

        mine = left.at[col]
        remote(mine, mine, l_send, l_far, row, far).start()
        each(1, 16, lambda k: remote(mine, mine, l_send, l_recv, row, plane_peer(col, k)).start())

        for half in range(2):
            for low in range(2):
                t_row, t_col = turn(half, low)

                @pl.when((t_row != row) | (t_col != col))
                def _():
                    wait_bytes(halves.at[half], r_send0.at[2 * half + low])
        for n in range(4):
            @pl.when((turn_row != row) | (turn_col + n != col))
            def _():
                wait_bytes(right.at[0], r_recv0.at[n])

    with jax.named_scope("spread"):
        four = right.at[pl.ds(turn_col, 4)]
        each(1, 4, lambda k: remote(
            four, four, r_send, r_relay.at[lax.rem(row, 8) // 2],
            (row // 8) * 8 + lax.rem(row + 2 * k, 8), col).start())
        remote(four, four, r_send, r_recv, sibling, col).start()

    with jax.named_scope("farwait"):
        far_block = left.at[far]
        wait_bytes(far_block, l_far)
        each(1, 16, lambda k: remote(
            far_block, far_block, l_send, l_recv, row, plane_peer(col, k)).start())

    def along_cols(buf, send_sem, recv_sem):
        for n, shift in enumerate(SHIFTS):
            @pl.when(on_map(col + shift))
            def _():
                remote(
                    buf.at[7], buf.at[7 - shift], send_sem.at[n], recv_sem.at[n], row, col + shift
                ).start()

            @pl.when(jnp.logical_not(on_map(col - shift)))
            def _():
                buf[7 - shift] = jnp.zeros((128, 128), BF)

    def wait_cols(buf, send_sem, recv_sem):
        for n, shift in enumerate(SHIFTS):
            @pl.when(on_map(col - shift))
            def _():
                wait_bytes(buf.at[7], recv_sem.at[n])
        for n, shift in enumerate(SHIFTS):
            @pl.when(on_map(col + shift))
            def _():
                wait_bytes(buf.at[7], send_sem.at[n])

    def along_rows(buf, send_sem, recv_sem):
        band = buf.at[pl.ds(5, 5)]
        none = jnp.zeros((5, 128, 128), BF)

        @pl.when(row < ROWS - 1)
        def _():
            remote(band, buf.at[pl.ds(0, 5)], send_sem.at[0], recv_sem.at[0], row + 1, col).start()

        @pl.when(row > 0)
        def _():
            remote(band, buf.at[pl.ds(10, 5)], send_sem.at[1], recv_sem.at[1], row - 1, col).start()

        @pl.when(row == 0)
        def _():
            buf[pl.ds(0, 5)] = none

        @pl.when(row == ROWS - 1)
        def _():
            buf[pl.ds(10, 5)] = none

    def wait_rows(buf, send_sem, recv_sem):
        @pl.when(row < ROWS - 1)
        def _():
            wait_bytes(buf.at[pl.ds(5, 5)], send_sem.at[0])
            wait_bytes(buf.at[pl.ds(10, 5)], recv_sem.at[1])

        @pl.when(row > 0)
        def _():
            wait_bytes(buf.at[pl.ds(5, 5)], send_sem.at[1])
            wait_bytes(buf.at[pl.ds(0, 5)], recv_sem.at[0])

    with jax.named_scope("relay"):
        def relay(k):
            p = lax.rem(row + ROWS - 2 * k, 8)
            block = right.at[pl.ds(4 * p, 4)]
            wait_bytes(block, r_relay.at[p // 2])
            remote(block, block, r_send, r_recv, sibling, col).start()

        each(1, 4, relay)
    along_cols(cots, c_send, c_recv)

    with jax.named_scope("cotangent"):
        for n in range(4, 10):
            loads[n].wait()
        gating = jax.nn.sigmoid(jnp.dot(normed, wgate_v[...], preferred_element_type=F32))

    one_rate = rates_s[0]
    two_rate = rates_s[1]
    to = lax.broadcasted_iota(jnp.int32, (128, 128), 0)
    at = lax.broadcasted_iota(jnp.int32, (128, 128), 1)
    flip = ((lax.rem(to, 16) * 8 + to // 16) == at).astype(BF)
    flip_back = ((lax.rem(to, 8) * 16 + to // 8) == at).astype(BF)

    def unfold(src, dst, blocks):
        for n in blocks:
            dr, dc = n // 5 - 1, n % 5 - 2
            inside = (row + dr >= 0) & (row + dr < ROWS) & (col + dc >= 0) & (col + dc < COLS)
            cell = jnp.dot(flip, src[n], preferred_element_type=F32)
            dst[pl.ds((dc + 2) * 8, 8), pl.ds((dr + 1) * 16, 16), :] = jnp.where(
                inside, cell, 0.0
            ).reshape(8, 16, 128)

    def back(value):
        return jnp.dot(flip_back, value, preferred_element_type=F32).astype(BF)

    with jax.named_scope("gatherwait"):
        wait_bytes(right.at[pl.ds(0, 16)], r_recv)
    with jax.named_scope("leftwait"):
        wait_bytes(left.at[pl.ds(0, 30)], l_recv)
        wait_cols(cots, c_send, c_recv)
        along_rows(cots, c_send2, c_recv2)

    with jax.named_scope("products"):
        for part in range(4):
            def add(c, total):
                a = left[c, pl.ds(part * 32, 32), :].astype(F32).reshape(4, 1, 8, 128)
                b = right[c].astype(F32).reshape(1, 8, 8, 128)
                return total + a * b

            total = lax.fori_loop(0, COLS, add, jnp.zeros((4, 8, 8, 128), F32))
            sums[pl.ds(part * 32, 32), :] = jnp.sum(total, axis=2).reshape(32, 128)

    with jax.named_scope("update"):
        product_norm = layer_norm(sums[...]).astype(BF)
        updated = (
            pair + gating * jnp.dot(product_norm, wout_v[...], preferred_element_type=F32)
        ).astype(BF).astype(F32)
        contact = mask_column(cmask_v[...])
        centre = updated - jnp.mean(updated, axis=-1, keepdims=True)
        inv = lax.rsqrt(jnp.mean(centre * centre, axis=-1, keepdims=True) + EPSILON)
        scaled = centre * inv
        first[7] = (scaled * contact).astype(BF)
    with jax.named_scope("rimcols"):
        along_cols(first, f_send, f_recv)
        wait_rows(cots, c_send2, c_recv2)
    with jax.named_scope("hidden"):
        unfold(cots, cfield, range(15))
        shifted(cfield, ctaps, 8, two_rate, 32, -1)
        back_two = jnp.concatenate([two_v[t].T for t in range(9)], axis=0)
        ghid[...] = jnp.dot(
            windows(ctaps, 8, two_rate, 24, -1), back_two, preferred_element_type=F32
        )
    with jax.named_scope("rimwait"):
        wait_cols(first, f_send, f_recv)
        along_rows(first, f_send2, f_recv2)
    with jax.named_scope("rimrows"):
        unfold(first, field, range(5, 10))
        wait_rows(first, f_send2, f_recv2)
    with jax.named_scope("unfold"):
        unfold(first, field, [*range(5), *range(10, 15)])
        shifted(field, taps, 8, one_rate, 32, 1)
    with jax.named_scope("conv"):
        pre = jnp.dot(
            windows(taps, 8, one_rate, 24, 1), one_v[...].reshape(1152, 128),
            preferred_element_type=F32,
        )
        c_at = lax.broadcasted_iota(jnp.int32, (24, 32, 128), 0) + (col * 8 - 8)
        r_at = lax.broadcasted_iota(jnp.int32, (24, 32, 128), 1) + (row * 16 - 8)
        inside = (c_at >= 0) & (c_at < 256) & (r_at >= 0) & (r_at < 256)
        sigma = jax.nn.sigmoid(pre)
        hidden[...] = jnp.where(inside, (pre * sigma).reshape(24, 32, 128), 0.0)
        gpre[...] = jnp.where(
            inside, (ghid[...] * sigma * (1.0 + pre * (1.0 - sigma))).reshape(24, 32, 128), 0.0
        )
        shifted(hidden, htaps, 8, two_rate, 16, 1)
    over = (((0,), (0,)), ((), ()))

    def scatter(k, low):
        peer = plane_peer(col, k)
        slot = plane_slot(peer)

        @pl.when((slot >= low) & (slot < low + 8))
        def _():
            remote(grads.at[slot], parts.at[me], send1, recv1, row, peer).start()

    with jax.named_scope("gradtwo"):
        cot_own = cots[7]
        second_taps = back(windows(htaps, 8, two_rate, 8, 1))
        grads[pl.ds(8, 8)] = lax.dot_general(
            second_taps, cot_own, over, preferred_element_type=F32
        ).astype(BF).reshape(8, 144, 128)
        each(1, 16, lambda k: scatter(k, 8))
    with jax.named_scope("gradone"):
        gpre_own = gpre[pl.ds(8, 8), pl.ds(8, 16), :].reshape(128, 128).astype(BF)
        first_taps = windows(taps, 16, one_rate, 8, 1, pl.ds(8, 16))
        grads[pl.ds(0, 8)] = lax.dot_general(
            first_taps, gpre_own, over, preferred_element_type=F32
        ).astype(BF).reshape(8, 144, 128)
        each(1, 16, lambda k: scatter(k, 0))
    with jax.named_scope("outputs"):
        parts[me] = grads[me]
        second_pre = jnp.dot(
            second_taps, two_v[...].reshape(1152, 128), preferred_element_type=F32
        )
        output_ref[...] = (updated + second_pre).astype(BF)
        shifted(gpre, gtaps, 8, one_rate, 16, -1)
        back_one = jnp.concatenate([one_v[t].T for t in range(9)], axis=0)
        grad_in = contact * jnp.dot(
            back(windows(gtaps, 8, one_rate, 8, -1)), back_one, preferred_element_type=F32
        )
        grad_norm = inv * (
            grad_in
            - jnp.mean(grad_in, axis=-1, keepdims=True)
            - scaled * jnp.mean(grad_in * scaled, axis=-1, keepdims=True)
        )
        gpair_ref[...] = (cot_own.astype(F32) + grad_norm).astype(BF)

    most = parts.at[pl.ds(0, 15)]
    with jax.named_scope("scatterwait"):
        wait_bytes(most, recv1)
    with jax.named_scope("addparts"):
        total = parts[0].astype(F32)
        for n in range(1, 16):
            total = total + parts[n].astype(F32)
        own[...] = total.astype(BF).reshape(9, 16, 128)
        for j in range(9):
            @pl.when(place != 3 * j)
            def _():
                remote(own.at[j], pieces.at[place], send2, recv2, *line(3 * j)).start()

    owner = (lax.rem(place, 3) == 0) & (place < 27)
    piece = place // 3

    with jax.named_scope("line"):
        @pl.when(owner)
        def _():
            pieces[place] = own[piece]
            wait_bytes(own.at[pl.ds(0, 8)], send2)
            wait_bytes(pieces.at[pl.ds(0, 31)], recv2)
            total = pieces[0].astype(F32)
            for n in range(1, 32):
                total = total + pieces[n].astype(F32)
            final[me, piece] = total.astype(BF)
            block = final.at[me, piece]
            each(1, 32, lambda k: remote(
                block, block, send3, recv3, *line(lax.rem(place + k, 32))).start())
            wait_bytes(own.at[pl.ds(0, 8)], recv3)

        @pl.when(jnp.logical_not(owner))
        def _():
            wait_bytes(own, send2)
            wait_bytes(own, recv3)

    with jax.named_scope("gather"):
        whole = final.at[me]
        each(1, 16, lambda k: remote(whole, whole, send4, recv4, row, plane_peer(col, k)).start())
        wait_bytes(right.at[pl.ds(0, 28)], r_send)
        wait_bytes(left.at[pl.ds(0, 31)], l_send)
        wait_bytes(most, send1)

        @pl.when(owner)
        def _():
            wait_bytes(pieces.at[pl.ds(0, 31)], send3)

        wait_bytes(final.at[pl.ds(0, 15)], recv4)
    with jax.named_scope("finish"):
        wait_bytes(final.at[pl.ds(0, 15)], send4)
        total_ref[...] = final[...].reshape(16, 144, 128)


VMEM = pltpu.VMEM
DMA = pltpu.SemaphoreType.DMA


def shape(dims, dtype):
    return jax.ShapeDtypeStruct(dims, dtype)


def local(
    pair, pair_mask, contact_mask, dilations, w_proj, w_gate, w_out, conv_one, conv_two, cotangent
):
    inputs = (
        pair.reshape(128, 128), pair_mask.T, contact_mask.T, dilations, w_proj, w_gate, w_out,
        conv_one, conv_two, cotangent.reshape(128, 128),
    )
    output, grad_pair, total = pl.pallas_call(
        kernel,
        out_shape=(shape((128, 128), BF), shape((128, 128), BF), shape((16, 144, 128), BF)),
        in_specs=[pl.BlockSpec(memory_space=pltpu.HBM)] * 10,
        out_specs=(pl.BlockSpec(memory_space=pltpu.VMEM),) * 3,
        scratch_shapes=[
            VMEM((128, 128), BF), VMEM((8, 16), jnp.int32), VMEM((8, 16), jnp.int32),
            pltpu.SMEM((2,), jnp.int32), VMEM((128, 512), BF), VMEM((128, 128), BF),
            VMEM((128, 128), BF), VMEM((9, 128, 128), BF), VMEM((9, 128, 128), BF), DMA((10,)),
            VMEM((32, 128, 128), BF), VMEM((32, 64, 128), BF), VMEM((2, 64, 128), BF),
            VMEM((15, 128, 128), BF), VMEM((15, 128, 128), BF), VMEM((128, 128), F32),
            VMEM((40, 48, 128), F32), VMEM((3, 40, 32, 128), BF),
            VMEM((40, 48, 128), F32), VMEM((3, 40, 32, 128), BF),
            VMEM((24, 32, 128), F32), VMEM((3, 24, 16, 128), BF),
            VMEM((24, 32, 128), F32), VMEM((3, 24, 16, 128), BF), VMEM((768, 128), F32),
            VMEM((16, 144, 128), BF), VMEM((16, 144, 128), BF), VMEM((9, 16, 128), BF),
            VMEM((32, 16, 128), BF), VMEM((16, 9, 16, 128), BF),
            DMA, DMA, DMA, DMA((4,)), DMA((4,)), DMA, DMA, DMA((4,)),
            DMA((4,)), DMA((4,)), DMA((2,)), DMA((2,)),
            DMA((4,)), DMA((4,)), DMA((2,)), DMA((2,)),
            DMA, DMA, DMA, DMA, DMA, DMA, DMA, DMA,
        ],
        compiler_params=pltpu.CompilerParams(
            collective_id=1, has_side_effects=True, vmem_limit_bytes=62 << 20
        ),
    )(*inputs)
    total = total.reshape(2, 9, 128, 128).astype(F32) * (1.0 / 256.0)
    return (output.reshape(16, 8, 128), grad_pair.reshape(16, 8, 128), total[0], total[1])


def solution(mesh):
    in_specs = (
        P("row", "col", None), P("row", "col"), P("row", "col"), P(), P(), P(), P(), P(), P(),
        P("row", "col", None),
    )
    out_specs = (P("row", "col", None), P("row", "col", None), P(), P())
    return jax.shard_map(local, mesh=mesh, in_specs=in_specs, out_specs=out_specs, check_vma=False)
```

time: 1220 us -> 102 us (0.08)
  waiting for transfers between devices: 1120 us -> 0 us
  Pallas kernels: 0 us -> 98.1 us
  starting transfers between devices: 50 us -> 0 us
  between operations: 19.7 us -> 0.66 us
  local copies, waits for them, and re-layouts: 15.9 us -> 2.32 us
    psum x2 -> x0, waiting for transfers between devices: 720 us -> none  [the longest x1 505 us: local(): grad_one, grad_two = lax.psum((grad_one, grad_two), ('row', 'col'))]
    all_gather x2 -> x0, waiting for transfers between devices: 397 us -> none  [the longest x1 309 us: local(): lax.all_gather(left_side, 'col', axis=1, tiled=True)]
    pallas_call x0 -> x1, Pallas kernels: none -> 98.1 us  [local(): pl.pallas_call(kernel, out_shape=(shape((128, 128), BF), shape((128, 128)...]
    ppermute x16 -> x0, starting transfers between devices: 49.8 us -> none  [the longest x8 32.4 us: with_halo(): lax.ppermute(lax.slice_in_dim(block, block.shape[dim] - width, None, axis...]
  transfers between devices with their start and end apart: 20 -> 0, of which waited for: 8 -> 0; matrix products, arithmetic and copies ran while one was open for 1% -> 0% of each run, Pallas kernels for 0% -> 0%
where the time goes in v2:
time: 102 us
  Pallas kernels  98.1 us (96%)
  local copies, waits for them, and re-layouts  2.32 us (2%)
  other arithmetic  1.14 us (1%)
    pallas_call x1, Pallas kernels, local(): pl.pallas_call(kernel, out_shape=(shape((128, 128), BF), shape((128, 128)...  98.1 us

profile of v2, /device:TPU:1, one launch (start us, length us, event | category | flops | bytes accessed | tf_op | source)
XLA Modules:
  0.0 102.2 jit_solution(317799317361953243)
XLA Ops:
  0.6 98.1 %shard_map.129 = (bf16[128,128]{1,0:T(8,128)(2,1)}, bf16[128,128]{1,0:T(8,128)(2,1)}, bf16[16,144,128]{2,1,0:T(8,128)(2,1)}) custom-call(bf16[128,128]{1,0:T(8,128)(2,1)} %bitcast.10, s32[8,16]{1,0:T(8,128)} %bitcast.14, s32[8,16]{1,0:T(8,128)} %bitcast.15, s32[2]{0:T(128)} %rates_h.1, bf16[128,512]{1,0:T(8,128)(2,1)} %wproj_h.1, bf16[128,128]{1,0:T(8,128)(2,1)} %wgate_h.1, ...), custom_call_target="tpu_custom_call" | custom-call | tf_op jit(solution)/shard_map/pallas_call | solution.py:464
  98.7 1.1 %convert_multiply_fusion = f32[16,144,128]{2,1,0:T(8,128)S(1)} fusion(bf16[16,144,128]{2,1,0:T(8,128)(2,1)} %get-tuple-element.9), kind=kLoop, calls=%fused_computation | loop fusion | flops 589824 | bytes 1769472 | tf_op jit(solution)/shard_map/mul | solution.py:490
  99.8 0.0 copy-start.1
  99.9 0.0 copy-start
  99.9 1.1 %fusion = (f32[8,144,128]{2,1,0:T(8,128)}, f32[8,144,128]{2,1,0:T(8,128)}) fusion(f32[16,144,128]{2,1,0:T(8,128)S(1)} %convert_multiply_fusion), kind=kLoop, calls=%fused_computation.1 | loop fusion | bytes 2359296 | tf_op jit(solution)/shard_map/slice | solution.py:491
  100.9 0.0 copy-done.1
  101.0 0.6 copy.16
  101.6 0.0 copy-done
  101.6 0.6 copy.17
Async XLA Ops:
  99.8 1.1 %copy-start.1 = (bf16[128,128]{1,0:T(8,128)(2,1)S(1)}, bf16[128,128]{1,0:T(8,128)(2,1)}, u32[]{:S(2)}) copy-start(bf16[128,128]{1,0:T(8,128)(2,1)} %get-tuple-element.7) | copy-start | bytes 98308
  99.9 1.7 %copy-start = (bf16[128,128]{1,0:T(8,128)(2,1)S(1)}, bf16[128,128]{1,0:T(8,128)(2,1)}, u32[]{:S(2)}) copy-start(bf16[128,128]{1,0:T(8,128)(2,1)} %get-tuple-element.8) | copy-start | bytes 98308

commit v3 on v2

--- a/solution.py
+++ b/solution.py
@@ -93,10 +93,10 @@
     pair_v, pmask_v, cmask_v, rates_s, wproj_v, wgate_v, wout_v, one_v, two_v, in_sem,
     left, right, halves, first, cots, sums,
     field, taps, cfield, ctaps, hidden, htaps, gpre, gtaps, ghid,
-    grads, parts, own, pieces, final,
-    l_send, l_recv, l_far, r_send0, r_recv0, r_send, r_recv, r_relay,
+    grads, parts, near, apart, final, partial,
+    l_send, l_recv, l_recv2, l_far, r_send0, r_recv0, r_send, r_recv, r_relay,
     c_send, c_recv, c_send2, c_recv2, f_send, f_recv, f_send2, f_recv2,
-    send1, recv1, send2, recv2, send3, recv3, send4, recv4,
+    send1, recv1, send2, recv2, send3, recv3, send4, recv4, recv5,
 ):
     row = lax.axis_index("row")
     col = lax.axis_index("col")
@@ -104,12 +104,18 @@
     sibling = row + 1 - 2 * lax.rem(row, 2)
     turn_row = col // 2
     turn_col = 4 * lax.rem(row, 8)
-    me = plane_slot(col)
-    place = row * 2 + lax.rem(col // 4, 2)
-    base = (col // 8) * 8 + lax.rem(col, 4)
-
-    def line(q):
-        return q // 2, base + lax.rem(q, 2) * 4
+    core = lax.rem(row, 2)
+    z_hi = lax.rem(col // 4, 2)
+    near_place = lax.rem(row // 2, 4)
+    far_place = z_hi * 2 + row // 8
+    me = core * 16 + plane_slot(col)
+
+    def near_row(k):
+        return (row // 8) * 8 + lax.rem(row + 2 * k, 8)
+
+    def far_at(k):
+        z = lax.rem(z_hi * 8 + row // 2 + 4 * k, 16)
+        return lax.rem(z, 8) * 2 + core, (col // 8) * 8 + (z // 8) * 4 + lax.rem(col, 4)
 
     with jax.named_scope("start"):
         loads = [
@@ -123,8 +129,17 @@
         for load in loads:
             load.start()
         barrier = pltpu.get_barrier_semaphore()
+        each(0, 16, lambda k: signal(barrier, sibling, plane_peer(col, k)))
         each(1, 16, lambda k: signal(barrier, row, plane_peer(col, k)))
-        each(1, 32, lambda k: signal(barrier, *line(lax.rem(place + k, 32))))
+        for k in range(1, 4):
+            signal(barrier, near_row(k), col)
+            signal(barrier, *far_at(k))
+        beside = row + 2 * core - 1
+
+        @pl.when((beside >= 0) & (beside < ROWS))
+        def _():
+            signal(barrier, beside, col)
+
         for shift in (1, 2, -1, -2):
             @pl.when(on_map(col + shift))
             def _():
@@ -153,7 +168,11 @@
         fixed = (turn_row == row) & (lax.rem(row, 8) == col // 4)
         pl.semaphore_wait(
             barrier,
-            50 - jnp.where(fixed, 1, 0) + jnp.minimum(col, 2) + jnp.minimum(COLS - 1 - col, 2),
+            41
+            - jnp.where(fixed, 1, 0)
+            + jnp.where((beside >= 0) & (beside < ROWS), 1, 0)
+            + jnp.minimum(col, 2)
+            + jnp.minimum(COLS - 1 - col, 2),
         )
 
     with jax.named_scope("turn"):
@@ -202,7 +221,7 @@
         far_block = left.at[far]
         wait_bytes(far_block, l_far)
         each(1, 16, lambda k: remote(
-            far_block, far_block, l_send, l_recv, row, plane_peer(col, k)).start())
+            far_block, far_block, l_send, l_recv2, row, plane_peer(col, k)).start())
 
     def along_cols(buf, send_sem, recv_sem):
         for n, shift in enumerate(SHIFTS):
@@ -291,21 +310,35 @@
     def back(value):
         return jnp.dot(flip_back, value, preferred_element_type=F32).astype(BF)
 
-    with jax.named_scope("gatherwait"):
-        wait_bytes(right.at[pl.ds(0, 16)], r_recv)
-    with jax.named_scope("leftwait"):
-        wait_bytes(left.at[pl.ds(0, 30)], l_recv)
+    sibling_part = right.at[pl.ds(0, 16)]
+
+    def add_from(half, part, total):
+        def add(n, total):
+            c = (n // 4) * 8 + half * 4 + lax.rem(n, 4)
+            a = left[c, pl.ds(part * 32, 32), :].astype(F32).reshape(4, 1, 8, 128)
+            b = right[c].astype(F32).reshape(1, 8, 8, 128)
+            return total + a * b
+
+        return lax.fori_loop(0, 16, add, total)
+
+    with jax.named_scope("products"):
+        @pl.when(core != z_hi)
+        def _():
+            wait_bytes(sibling_part, r_recv)
+
+        wait_bytes(left.at[pl.ds(0, 15)], l_recv)
+        for part in range(4):
+            partial[part] = add_from(z_hi, part, jnp.zeros((4, 8, 8, 128), F32))
+        wait_bytes(left.at[pl.ds(0, 15)], l_recv2)
+
+        @pl.when(core == z_hi)
+        def _():
+            wait_bytes(sibling_part, r_recv)
+
         wait_cols(cots, c_send, c_recv)
         along_rows(cots, c_send2, c_recv2)
-
-    with jax.named_scope("products"):
         for part in range(4):
-            def add(c, total):
-                a = left[c, pl.ds(part * 32, 32), :].astype(F32).reshape(4, 1, 8, 128)
-                b = right[c].astype(F32).reshape(1, 8, 8, 128)
-                return total + a * b
-
-            total = lax.fori_loop(0, COLS, add, jnp.zeros((4, 8, 8, 128), F32))
+            total = add_from(1 - z_hi, part, partial[part])
             sums[pl.ds(part * 32, 32), :] = jnp.sum(total, axis=2).reshape(32, 128)
 
     with jax.named_scope("update"):
@@ -353,28 +386,36 @@
         shifted(hidden, htaps, 8, two_rate, 16, 1)
     over = (((0,), (0,)), ((), ()))
 
-    def scatter(k, low):
-        peer = plane_peer(col, k)
-        slot = plane_slot(peer)
-
-        @pl.when((slot >= low) & (slot < low + 8))
-        def _():
-            remote(grads.at[slot], parts.at[me], send1, recv1, row, peer).start()
+    def scatter(there):
+        def one(k):
+            peer = plane_peer(col, k)
+
+            @pl.when((k > 0) | (there != core))
+            def _():
+                remote(
+                    grads.at[there * 16 + plane_slot(peer)], parts.at[me], send1, recv1,
+                    row - core + there, peer,
+                ).start()
+
+        each(0, 16, one)
+
+    def padded(value):
+        return jnp.concatenate([value.astype(BF), jnp.zeros((128, 128), BF)]).reshape(16, 80, 128)
 
     with jax.named_scope("gradtwo"):
         cot_own = cots[7]
         second_taps = back(windows(htaps, 8, two_rate, 8, 1))
-        grads[pl.ds(8, 8)] = lax.dot_general(
-            second_taps, cot_own, over, preferred_element_type=F32
-        ).astype(BF).reshape(8, 144, 128)
-        each(1, 16, lambda k: scatter(k, 8))
+        grads[pl.ds(16, 16)] = padded(
+            lax.dot_general(second_taps, cot_own, over, preferred_element_type=F32)
+        )
+        scatter(1)
     with jax.named_scope("gradone"):
         gpre_own = gpre[pl.ds(8, 8), pl.ds(8, 16), :].reshape(128, 128).astype(BF)
         first_taps = windows(taps, 16, one_rate, 8, 1, pl.ds(8, 16))
-        grads[pl.ds(0, 8)] = lax.dot_general(
-            first_taps, gpre_own, over, preferred_element_type=F32
-        ).astype(BF).reshape(8, 144, 128)
-        each(1, 16, lambda k: scatter(k, 0))
+        grads[pl.ds(0, 16)] = padded(
+            lax.dot_general(first_taps, gpre_own, over, preferred_element_type=F32)
+        )
+        scatter(0)
     with jax.named_scope("outputs"):
         parts[me] = grads[me]
         second_pre = jnp.dot(
@@ -393,57 +434,59 @@
         )
         gpair_ref[...] = (cot_own.astype(F32) + grad_norm).astype(BF)
 
-    most = parts.at[pl.ds(0, 15)]
+    def added(buf, count):
+        total = buf[0].astype(F32)
+        for n in range(1, count):
+            total = total + buf[n].astype(F32)
+        return total.astype(BF)
+
+    most = parts.at[pl.ds(0, 31)]
+    three = near.at[pl.ds(0, 3)]
     with jax.named_scope("scatterwait"):
         wait_bytes(most, recv1)
-    with jax.named_scope("addparts"):
-        total = parts[0].astype(F32)
-        for n in range(1, 16):
-            total = total + parts[n].astype(F32)
-        own[...] = total.astype(BF).reshape(9, 16, 128)
-        for j in range(9):
-            @pl.when(place != 3 * j)
-            def _():
-                remote(own.at[j], pieces.at[place], send2, recv2, *line(3 * j)).start()
-
-    owner = (lax.rem(place, 3) == 0) & (place < 27)
-    piece = place // 3
-
-    with jax.named_scope("line"):
-        @pl.when(owner)
-        def _():
-            pieces[place] = own[piece]
-            wait_bytes(own.at[pl.ds(0, 8)], send2)
-            wait_bytes(pieces.at[pl.ds(0, 31)], recv2)
-            total = pieces[0].astype(F32)
-            for n in range(1, 32):
-                total = total + pieces[n].astype(F32)
-            final[me, piece] = total.astype(BF)
-            block = final.at[me, piece]
-            each(1, 32, lambda k: remote(
-                block, block, send3, recv3, *line(lax.rem(place + k, 32))).start())
-            wait_bytes(own.at[pl.ds(0, 8)], recv3)
-
-        @pl.when(jnp.logical_not(owner))
-        def _():
-            wait_bytes(own, send2)
-            wait_bytes(own, recv3)
-
+    with jax.named_scope("near"):
+        near[near_place] = added(parts, 32)
+        block = near.at[near_place]
+        for k in range(1, 4):
+            remote(block, block, send2, recv2, near_row(k), col).start()
+        wait_bytes(three, recv2)
+    with jax.named_scope("apart"):
+        apart[far_place] = added(near, 4)
+        block_far = apart.at[far_place]
+        for k in (2, 1, 3):
+            remote(block_far, block_far, send3, recv3, *far_at(k)).start()
+        wait_bytes(three, recv3)
     with jax.named_scope("gather"):
+        final[me] = added(apart, 4)
         whole = final.at[me]
-        each(1, 16, lambda k: remote(whole, whole, send4, recv4, row, plane_peer(col, k)).start())
+        each(1, 16, lambda k: remote(
+            whole, whole, send4, recv4.at[plane_slot(col)], row, plane_peer(col, k)).start())
+        remote(whole, whole, send4, recv5, sibling, col).start()
+
+        def hand_on(k):
+            slot = plane_slot(plane_peer(col, k))
+            block = final.at[core * 16 + slot]
+            wait_bytes(block, recv4.at[slot])
+            remote(block, block, send4, recv5, sibling, col).start()
+
+        each(1, 16, hand_on)
         wait_bytes(right.at[pl.ds(0, 28)], r_send)
         wait_bytes(left.at[pl.ds(0, 31)], l_send)
         wait_bytes(most, send1)
-
-        @pl.when(owner)
-        def _():
-            wait_bytes(pieces.at[pl.ds(0, 31)], send3)
-
-        wait_bytes(final.at[pl.ds(0, 15)], recv4)
+        wait_bytes(three, send2)
+        wait_bytes(three, send3)
+        wait_bytes(final.at[pl.ds(0, 16)], recv5)
     with jax.named_scope("finish"):
-        wait_bytes(final.at[pl.ds(0, 15)], send4)
-        total_ref[...] = final[...].reshape(16, 144, 128)
+        wait_bytes(most, send4)
+        total_ref[...] = final[...]
+
+
+def finish_kernel(output_in, gpair_in, total_in, output_ref, gpair_ref, one_ref, two_ref):
+    output_ref[...] = output_in[...]
+    gpair_ref[...] = gpair_in[...]
+    for half, ref in enumerate((one_ref, two_ref)):
+        grad = total_in[pl.ds(16 * half, 16)].reshape(1280, 128)[:1152].astype(F32)
+        ref[...] = (grad * (1.0 / 256.0)).reshape(9, 128, 128)
 
 
 VMEM = pltpu.VMEM
@@ -463,7 +506,7 @@
     )
     output, grad_pair, total = pl.pallas_call(
         kernel,
-        out_shape=(shape((128, 128), BF), shape((128, 128), BF), shape((16, 144, 128), BF)),
+        out_shape=(shape((128, 128), BF), shape((128, 128), BF), shape((32, 80, 128), BF)),
         in_specs=[pl.BlockSpec(memory_space=pltpu.HBM)] * 10,
         out_specs=(pl.BlockSpec(memory_space=pltpu.VMEM),) * 3,
         scratch_shapes=[
@@ -476,19 +519,28 @@
             VMEM((40, 48, 128), F32), VMEM((3, 40, 32, 128), BF),
             VMEM((24, 32, 128), F32), VMEM((3, 24, 16, 128), BF),
             VMEM((24, 32, 128), F32), VMEM((3, 24, 16, 128), BF), VMEM((768, 128), F32),
-            VMEM((16, 144, 128), BF), VMEM((16, 144, 128), BF), VMEM((9, 16, 128), BF),
-            VMEM((32, 16, 128), BF), VMEM((16, 9, 16, 128), BF),
-            DMA, DMA, DMA, DMA((4,)), DMA((4,)), DMA, DMA, DMA((4,)),
+            VMEM((32, 80, 128), BF), VMEM((32, 80, 128), BF), VMEM((4, 80, 128), BF),
+            VMEM((4, 80, 128), BF), VMEM((32, 80, 128), BF), VMEM((4, 4, 8, 8, 128), F32),
+            DMA, DMA, DMA, DMA, DMA((4,)), DMA((4,)), DMA, DMA, DMA((4,)),
             DMA((4,)), DMA((4,)), DMA((2,)), DMA((2,)),
             DMA((4,)), DMA((4,)), DMA((2,)), DMA((2,)),
-            DMA, DMA, DMA, DMA, DMA, DMA, DMA, DMA,
+            DMA, DMA, DMA, DMA, DMA, DMA, DMA, DMA((16,)), DMA,
         ],
         compiler_params=pltpu.CompilerParams(
             collective_id=1, has_side_effects=True, vmem_limit_bytes=62 << 20
         ),
     )(*inputs)
-    total = total.reshape(2, 9, 128, 128).astype(F32) * (1.0 / 256.0)
-    return (output.reshape(16, 8, 128), grad_pair.reshape(16, 8, 128), total[0], total[1])
+    whole = pl.BlockSpec(memory_space=pltpu.VMEM)
+    output, grad_pair, grad_one, grad_two = pl.pallas_call(
+        finish_kernel,
+        out_shape=(
+            shape((128, 128), BF), shape((128, 128), BF),
+            shape((9, 128, 128), F32), shape((9, 128, 128), F32),
+        ),
+        in_specs=[whole] * 3,
+        out_specs=(whole,) * 4,
+    )(output, grad_pair, total)
+    return (output.reshape(16, 8, 128), grad_pair.reshape(16, 8, 128), grad_one, grad_two)
 
 
 def solution(mesh):

time: 102 us -> 98.2 us (0.963)
  local copies, waits for them, and re-layouts: 2.32 us -> 0 us
  other arithmetic: 1.14 us -> 0 us
    pallas_call x1, Pallas kernels: 98.1 us -> 95.3 us  [local(): pl.pallas_call(kernel, out_shape=(shape((128, 128), BF), shape((128, 128)...]
    pallas_call x0 -> x1, Pallas kernels: none -> 2.18 us  [local(): pl.pallas_call(finish_kernel, out_shape=(shape((128, 128), BF), shape((12...]
    unnamed x6 -> x0, local copies, waits for them, and re-layouts: 1.24 us -> none
    mul x1 -> x0, other arithmetic: 1.14 us -> none  [local(): total = total.reshape(2, 9, 128, 128).astype(F32) * (1.0 / 256.0)]
    slice x1 -> x0, local copies, waits for them, and re-layouts: 1.09 us -> none  [local(): total[1]]
where the time goes in v3:
time: 98.2 us; the launch traced here: 98.1 us
  Pallas kernels  97.4 us (99%)
    pallas_call x1, Pallas kernels, local(): pl.pallas_call(kernel, out_shape=(shape((128, 128), BF), shape((128, 128)...  95.3 us
    pallas_call x1, Pallas kernels, local(): pl.pallas_call(finish_kernel, out_shape=(shape((128, 128), BF), shape((12...  2.18 us

profile of v3, /device:TPU:1, one launch (start us, length us, event | category | flops | bytes accessed | tf_op | source)
XLA Modules:
  0.0 98.1 jit_solution(9050352025414744241)
XLA Ops:
  0.6 95.3 %shard_map.129 = (bf16[128,128]{1,0:T(8,128)(2,1)}, bf16[128,128]{1,0:T(8,128)(2,1)}, bf16[32,80,128]{2,1,0:T(8,128)(2,1)}) custom-call(bf16[128,128]{1,0:T(8,128)(2,1)} %bitcast.6, s32[8,16]{1,0:T(8,128)} %bitcast.8, s32[8,16]{1,0:T(8,128)} %bitcast.9, s32[2]{0:T(128)} %rates_h.1, bf16[128,512]{1,0:T(8,128)(2,1)} %wproj_h.1, bf16[128,128]{1,0:T(8,128)(2,1)} %wgate_h.1, ...), custom_call_target="tpu_custom_call" | custom-call | tf_op jit(solution)/shard_map/pallas_call | solution.py:507
  95.9 2.2 %shard_map.130 = (bf16[128,128]{1,0:T(8,128)(2,1)}, bf16[128,128]{1,0:T(8,128)(2,1)}, f32[9,128,128]{2,1,0:T(8,128)}, f32[9,128,128]{2,1,0:T(8,128)}) custom-call(bf16[128,128]{1,0:T(8,128)(2,1)} %get-tuple-element.11.output_in, bf16[128,128]{1,0:T(8,128)(2,1)} %get-tuple-element.12.gpair_in, bf16[32,80,128]{2,1,0:T(8,128)(2,1)} %get-tuple-element.13.total_in), custom_call_target="tpu_custom_call" | custom-call | tf_op jit(solution)/shard_map/pallas_call | solution.py:534

commit v4 on v3

--- a/solution.py
+++ b/solution.py
@@ -11,6 +11,7 @@
 F32 = jnp.float32
 ROWS = 16
 COLS = 32
+CHUNKS = (pl.ds(0, 48), pl.ds(48, 32))
 SHIFTS = (1, 2, -1, -2)
 
 
@@ -104,6 +105,7 @@
     sibling = row + 1 - 2 * lax.rem(row, 2)
     turn_row = col // 2
     turn_col = 4 * lax.rem(row, 8)
+    inward = jnp.where(lax.rem(col, 4) < 2, 1, -1)
     core = lax.rem(row, 2)
     z_hi = lax.rem(col // 4, 2)
     near_place = lax.rem(row // 2, 4)
@@ -175,6 +177,59 @@
             + jnp.minimum(COLS - 1 - col, 2),
         )
 
+    def along_cols(buf, send_sem, recv_sem):
+        for n, shift in enumerate(SHIFTS):
+            @pl.when(on_map(col + shift))
+            def _():
+                remote(
+                    buf.at[7], buf.at[7 - shift], send_sem.at[n], recv_sem.at[n], row, col + shift
+                ).start()
+
+            @pl.when(jnp.logical_not(on_map(col - shift)))
+            def _():
+                buf[7 - shift] = jnp.zeros((128, 128), BF)
+
+    def wait_cols(buf, send_sem, recv_sem):
+        for n, shift in enumerate(SHIFTS):
+            @pl.when(on_map(col - shift))
+            def _():
+                wait_bytes(buf.at[7], recv_sem.at[n])
+        for n, shift in enumerate(SHIFTS):
+            @pl.when(on_map(col + shift))
+            def _():
+                wait_bytes(buf.at[7], send_sem.at[n])
+
+    def along_rows(buf, send_sem, recv_sem):
+        band = buf.at[pl.ds(5, 5)]
+        none = jnp.zeros((5, 128, 128), BF)
+
+        @pl.when(row < ROWS - 1)
+        def _():
+            remote(band, buf.at[pl.ds(0, 5)], send_sem.at[0], recv_sem.at[0], row + 1, col).start()
+
+        @pl.when(row > 0)
+        def _():
+            remote(band, buf.at[pl.ds(10, 5)], send_sem.at[1], recv_sem.at[1], row - 1, col).start()
+
+        @pl.when(row == 0)
+        def _():
+            buf[pl.ds(0, 5)] = none
+
+        @pl.when(row == ROWS - 1)
+        def _():
+            buf[pl.ds(10, 5)] = none
+
+    def wait_rows(buf, send_sem, recv_sem):
+        @pl.when(row < ROWS - 1)
+        def _():
+            wait_bytes(buf.at[pl.ds(5, 5)], send_sem.at[0])
+            wait_bytes(buf.at[pl.ds(10, 5)], recv_sem.at[1])
+
+        @pl.when(row > 0)
+        def _():
+            wait_bytes(buf.at[pl.ds(5, 5)], send_sem.at[1])
+            wait_bytes(buf.at[pl.ds(0, 5)], recv_sem.at[0])
+
     with jax.named_scope("turn"):
         def turn(half, low):
             return low * 8 + col // 4, 2 * row + half
@@ -223,58 +278,7 @@
         each(1, 16, lambda k: remote(
             far_block, far_block, l_send, l_recv2, row, plane_peer(col, k)).start())
 
-    def along_cols(buf, send_sem, recv_sem):
-        for n, shift in enumerate(SHIFTS):
-            @pl.when(on_map(col + shift))
-            def _():
-                remote(
-                    buf.at[7], buf.at[7 - shift], send_sem.at[n], recv_sem.at[n], row, col + shift
-                ).start()
-
-            @pl.when(jnp.logical_not(on_map(col - shift)))
-            def _():
-                buf[7 - shift] = jnp.zeros((128, 128), BF)
-
-    def wait_cols(buf, send_sem, recv_sem):
-        for n, shift in enumerate(SHIFTS):
-            @pl.when(on_map(col - shift))
-            def _():
-                wait_bytes(buf.at[7], recv_sem.at[n])
-        for n, shift in enumerate(SHIFTS):
-            @pl.when(on_map(col + shift))
-            def _():
-                wait_bytes(buf.at[7], send_sem.at[n])
-
-    def along_rows(buf, send_sem, recv_sem):
-        band = buf.at[pl.ds(5, 5)]
-        none = jnp.zeros((5, 128, 128), BF)
-
-        @pl.when(row < ROWS - 1)
-        def _():
-            remote(band, buf.at[pl.ds(0, 5)], send_sem.at[0], recv_sem.at[0], row + 1, col).start()
-
-        @pl.when(row > 0)
-        def _():
-            remote(band, buf.at[pl.ds(10, 5)], send_sem.at[1], recv_sem.at[1], row - 1, col).start()
-
-        @pl.when(row == 0)
-        def _():
-            buf[pl.ds(0, 5)] = none
-
-        @pl.when(row == ROWS - 1)
-        def _():
-            buf[pl.ds(10, 5)] = none
-
-    def wait_rows(buf, send_sem, recv_sem):
-        @pl.when(row < ROWS - 1)
-        def _():
-            wait_bytes(buf.at[pl.ds(5, 5)], send_sem.at[0])
-            wait_bytes(buf.at[pl.ds(10, 5)], recv_sem.at[1])
-
-        @pl.when(row > 0)
-        def _():
-            wait_bytes(buf.at[pl.ds(5, 5)], send_sem.at[1])
-            wait_bytes(buf.at[pl.ds(0, 5)], recv_sem.at[0])
+    along_cols(cots, c_send, c_recv)
 
     with jax.named_scope("relay"):
         def relay(k):
@@ -284,8 +288,6 @@
             remote(block, block, r_send, r_recv, sibling, col).start()
 
         each(1, 4, relay)
-    along_cols(cots, c_send, c_recv)
-
     with jax.named_scope("cotangent"):
         for n in range(4, 10):
             loads[n].wait()
@@ -335,24 +337,61 @@
         def _():
             wait_bytes(sibling_part, r_recv)
 
+        contact = mask_column(cmask_v[...])
+        for half in range(2):
+            for part in (2 * half, 2 * half + 1):
+                total = add_from(1 - z_hi, part, partial[part])
+                sums[pl.ds(part * 32, 32), :] = jnp.sum(total, axis=2).reshape(32, 128)
+            rows = slice(64 * half, 64 * half + 64)
+            product_norm = layer_norm(sums[rows, :]).astype(BF)
+            new = (
+                pair[rows]
+                + gating[rows] * jnp.dot(product_norm, wout_v[...], preferred_element_type=F32)
+            ).astype(BF).astype(F32)
+            sums[rows, :] = new
+            first[7, rows, :] = (layer_norm(new) * contact[rows]).astype(BF)
+            for shift in (-inward, -2 * inward, inward, 2 * inward):
+                @pl.when(on_map(col + shift))
+                def _():
+                    block = pl.ds(64 * half, 64)
+                    remote(
+                        first.at[7, block], first.at[7 - shift, block], f_send.at[2 + shift],
+                        f_recv.at[2 - shift], row, col + shift,
+                    ).start()
+
+    with jax.named_scope("rimcols"):
+        for shift in SHIFTS:
+            @pl.when(jnp.logical_not(on_map(col - shift)))
+            def _():
+                first[7 - shift] = jnp.zeros((128, 128), BF)
+
+        def hand_rows(delta):
+            block = first.at[7 + delta]
+
+            @pl.when(row < ROWS - 1)
+            def _():
+                remote(
+                    block, first.at[2 + delta], f_send2.at[0], f_recv2.at[0, 2 + delta], row + 1, col
+                ).start()
+
+            @pl.when(row > 0)
+            def _():
+                remote(
+                    block, first.at[12 + delta], f_send2.at[1], f_recv2.at[1, 2 + delta], row - 1, col
+                ).start()
+
+        def take_column(delta):
+            @pl.when(on_map(col + delta))
+            def _():
+                wait_bytes(first.at[7], f_recv.at[2 + delta])
+
+            hand_rows(delta)
+
+        hand_rows(0)
         wait_cols(cots, c_send, c_recv)
         along_rows(cots, c_send2, c_recv2)
-        for part in range(4):
-            total = add_from(1 - z_hi, part, partial[part])
-            sums[pl.ds(part * 32, 32), :] = jnp.sum(total, axis=2).reshape(32, 128)
-
-    with jax.named_scope("update"):
-        product_norm = layer_norm(sums[...]).astype(BF)
-        updated = (
-            pair + gating * jnp.dot(product_norm, wout_v[...], preferred_element_type=F32)
-        ).astype(BF).astype(F32)
-        contact = mask_column(cmask_v[...])
-        centre = updated - jnp.mean(updated, axis=-1, keepdims=True)
-        inv = lax.rsqrt(jnp.mean(centre * centre, axis=-1, keepdims=True) + EPSILON)
-        scaled = centre * inv
-        first[7] = (scaled * contact).astype(BF)
-    with jax.named_scope("rimcols"):
-        along_cols(first, f_send, f_recv)
+        take_column(inward)
+        take_column(2 * inward)
         wait_rows(cots, c_send2, c_recv2)
     with jax.named_scope("hidden"):
         unfold(cots, cfield, range(15))
@@ -362,11 +401,32 @@
             windows(ctaps, 8, two_rate, 24, -1), back_two, preferred_element_type=F32
         )
     with jax.named_scope("rimwait"):
-        wait_cols(first, f_send, f_recv)
-        along_rows(first, f_send2, f_recv2)
+        take_column(-inward)
+        take_column(-2 * inward)
+        unfold(first, field, range(5, 10))
     with jax.named_scope("rimrows"):
-        unfold(first, field, range(5, 10))
-        wait_rows(first, f_send2, f_recv2)
+        for shift in SHIFTS:
+            @pl.when(on_map(col + shift))
+            def _():
+                wait_bytes(first.at[7], f_send.at[2 + shift])
+
+        for delta in range(5):
+            @pl.when(row < ROWS - 1)
+            def _():
+                wait_bytes(first.at[7], f_recv2.at[1, delta])
+
+            @pl.when(row > 0)
+            def _():
+                wait_bytes(first.at[7], f_recv2.at[0, delta])
+
+        @pl.when(row < ROWS - 1)
+        def _():
+            wait_bytes(first.at[pl.ds(0, 5)], f_send2.at[0])
+
+        @pl.when(row > 0)
+        def _():
+            wait_bytes(first.at[pl.ds(0, 5)], f_send2.at[1])
+
     with jax.named_scope("unfold"):
         unfold(first, field, [*range(5), *range(10, 15)])
         shifted(field, taps, 8, one_rate, 32, 1)
@@ -386,14 +446,15 @@
         shifted(hidden, htaps, 8, two_rate, 16, 1)
     over = (((0,), (0,)), ((), ()))
 
-    def scatter(there):
+    def scatter(there, chunk):
         def one(k):
             peer = plane_peer(col, k)
 
             @pl.when((k > 0) | (there != core))
             def _():
                 remote(
-                    grads.at[there * 16 + plane_slot(peer)], parts.at[me], send1, recv1,
+                    grads.at[there * 16 + plane_slot(peer), CHUNKS[chunk]],
+                    parts.at[me, CHUNKS[chunk]], send1, recv1.at[chunk],
                     row - core + there, peer,
                 ).start()
 
@@ -408,16 +469,22 @@
         grads[pl.ds(16, 16)] = padded(
             lax.dot_general(second_taps, cot_own, over, preferred_element_type=F32)
         )
-        scatter(1)
+        scatter(1, 0)
     with jax.named_scope("gradone"):
         gpre_own = gpre[pl.ds(8, 8), pl.ds(8, 16), :].reshape(128, 128).astype(BF)
         first_taps = windows(taps, 16, one_rate, 8, 1, pl.ds(8, 16))
         grads[pl.ds(0, 16)] = padded(
             lax.dot_general(first_taps, gpre_own, over, preferred_element_type=F32)
         )
-        scatter(0)
+        scatter(0, 0)
+        scatter(1, 1)
+        scatter(0, 1)
     with jax.named_scope("outputs"):
         parts[me] = grads[me]
+        updated = sums[...]
+        centre = updated - jnp.mean(updated, axis=-1, keepdims=True)
+        inv = lax.rsqrt(jnp.mean(centre * centre, axis=-1, keepdims=True) + EPSILON)
+        scaled = centre * inv
         second_pre = jnp.dot(
             second_taps, two_v[...].reshape(1152, 128), preferred_element_type=F32
         )
@@ -434,42 +501,46 @@
         )
         gpair_ref[...] = (cot_own.astype(F32) + grad_norm).astype(BF)
 
-    def added(buf, count):
-        total = buf[0].astype(F32)
+    def added(buf, count, chunk):
+        total = buf[0, CHUNKS[chunk], :].astype(F32)
         for n in range(1, count):
-            total = total + buf[n].astype(F32)
+            total = total + buf[n, CHUNKS[chunk], :].astype(F32)
         return total.astype(BF)
 
     most = parts.at[pl.ds(0, 31)]
     three = near.at[pl.ds(0, 3)]
-    with jax.named_scope("scatterwait"):
-        wait_bytes(most, recv1)
     with jax.named_scope("near"):
-        near[near_place] = added(parts, 32)
-        block = near.at[near_place]
-        for k in range(1, 4):
-            remote(block, block, send2, recv2, near_row(k), col).start()
-        wait_bytes(three, recv2)
+        for chunk, rows in enumerate(CHUNKS):
+            wait_bytes(parts.at[pl.ds(0, 31), rows], recv1.at[chunk])
+            near[near_place, rows, :] = added(parts, 32, chunk)
+            block = near.at[near_place, rows]
+            for k in range(1, 4):
+                remote(block, block, send2, recv2.at[chunk], near_row(k), col).start()
     with jax.named_scope("apart"):
-        apart[far_place] = added(near, 4)
-        block_far = apart.at[far_place]
-        for k in (2, 1, 3):
-            remote(block_far, block_far, send3, recv3, *far_at(k)).start()
-        wait_bytes(three, recv3)
+        for chunk, rows in enumerate(CHUNKS):
+            wait_bytes(near.at[pl.ds(0, 3), rows], recv2.at[chunk])
+            apart[far_place, rows, :] = added(near, 4, chunk)
+            block_far = apart.at[far_place, rows]
+            for k in (2, 1, 3):
+                remote(block_far, block_far, send3, recv3.at[chunk], *far_at(k)).start()
     with jax.named_scope("gather"):
-        final[me] = added(apart, 4)
-        whole = final.at[me]
-        each(1, 16, lambda k: remote(
-            whole, whole, send4, recv4.at[plane_slot(col)], row, plane_peer(col, k)).start())
-        remote(whole, whole, send4, recv5, sibling, col).start()
-
-        def hand_on(k):
-            slot = plane_slot(plane_peer(col, k))
-            block = final.at[core * 16 + slot]
-            wait_bytes(block, recv4.at[slot])
-            remote(block, block, send4, recv5, sibling, col).start()
-
-        each(1, 16, hand_on)
+        for chunk, rows in enumerate(CHUNKS):
+            wait_bytes(apart.at[pl.ds(0, 3), rows], recv3.at[chunk])
+            final[me, rows, :] = added(apart, 4, chunk)
+            whole = final.at[me, rows]
+            each(1, 16, lambda k: remote(
+                whole, whole, send4, recv4.at[chunk, plane_slot(col)], row, plane_peer(col, k)
+            ).start())
+            remote(whole, whole, send4, recv5, sibling, col).start()
+
+        for chunk, rows in enumerate(CHUNKS):
+            def hand_on(k):
+                slot = plane_slot(plane_peer(col, k))
+                block = final.at[core * 16 + slot, rows]
+                wait_bytes(block, recv4.at[chunk, slot])
+                remote(block, block, send4, recv5, sibling, col).start()
+
+            each(1, 16, hand_on)
         wait_bytes(right.at[pl.ds(0, 28)], r_send)
         wait_bytes(left.at[pl.ds(0, 31)], l_send)
         wait_bytes(most, send1)
@@ -523,8 +594,8 @@
             VMEM((4, 80, 128), BF), VMEM((32, 80, 128), BF), VMEM((4, 4, 8, 8, 128), F32),
             DMA, DMA, DMA, DMA, DMA((4,)), DMA((4,)), DMA, DMA, DMA((4,)),
             DMA((4,)), DMA((4,)), DMA((2,)), DMA((2,)),
-            DMA((4,)), DMA((4,)), DMA((2,)), DMA((2,)),
-            DMA, DMA, DMA, DMA, DMA, DMA, DMA, DMA((16,)), DMA,
+            DMA((5,)), DMA((5,)), DMA((2,)), DMA((2, 5)),
+            DMA, DMA((2,)), DMA, DMA((2,)), DMA, DMA((2,)), DMA, DMA((2, 16)), DMA,
         ],
         compiler_params=pltpu.CompilerParams(
             collective_id=1, has_side_effects=True, vmem_limit_bytes=62 << 20

time: 98.2 us -> 93 us (0.947)
  Pallas kernels: 97.4 us -> 92.2 us
    pallas_call x1, Pallas kernels: 95.3 us -> 90 us  [local(): pl.pallas_call(kernel, out_shape=(shape((128, 128), BF), shape((128, 128)...]
where the time goes in v4:
time: 93 us; the launch traced here: 92.9 us
  Pallas kernels  92.2 us (99%)
    pallas_call x1, Pallas kernels, local(): pl.pallas_call(kernel, out_shape=(shape((128, 128), BF), shape((128, 128)...  90 us
    pallas_call x1, Pallas kernels, local(): pl.pallas_call(finish_kernel, out_shape=(shape((128, 128), BF), shape((12...  2.18 us

profile of v4, /device:TPU:1, one launch (start us, length us, event | category | flops | bytes accessed | tf_op | source)
XLA Modules:
  0.0 92.9 jit_solution(5090276037501614391)
XLA Ops:
  0.6 90.0 %shard_map.129 = (bf16[128,128]{1,0:T(8,128)(2,1)}, bf16[128,128]{1,0:T(8,128)(2,1)}, bf16[32,80,128]{2,1,0:T(8,128)(2,1)}) custom-call(bf16[128,128]{1,0:T(8,128)(2,1)} %bitcast.6, s32[8,16]{1,0:T(8,128)} %bitcast.8, s32[8,16]{1,0:T(8,128)} %bitcast.9, s32[2]{0:T(128)} %rates_h.1, bf16[128,512]{1,0:T(8,128)(2,1)} %wproj_h.1, bf16[128,128]{1,0:T(8,128)(2,1)} %wgate_h.1, ...), custom_call_target="tpu_custom_call" | custom-call | tf_op jit(solution)/shard_map/pallas_call | solution.py:578
  90.7 2.2 %shard_map.130 = (bf16[128,128]{1,0:T(8,128)(2,1)}, bf16[128,128]{1,0:T(8,128)(2,1)}, f32[9,128,128]{2,1,0:T(8,128)}, f32[9,128,128]{2,1,0:T(8,128)}) custom-call(bf16[128,128]{1,0:T(8,128)(2,1)} %get-tuple-element.11.output_in, bf16[128,128]{1,0:T(8,128)(2,1)} %get-tuple-element.12.gpair_in, bf16[32,80,128]{2,1,0:T(8,128)(2,1)} %get-tuple-element.13.total_in), custom_call_target="tpu_custom_call" | custom-call | tf_op jit(solution)/shard_map/pallas_call | solution.py:605

commit v5 on v4

--- a/solution.py
+++ b/solution.py
@@ -120,6 +120,28 @@
         return lax.rem(z, 8) * 2 + core, (col // 8) * 8 + (z // 8) * 4 + lax.rem(col, 4)
 
     with jax.named_scope("start"):
+        barrier = pltpu.get_barrier_semaphore()
+        for k in (2, 1, 3):
+            signal(barrier, *far_at(k))
+        for n in range(4):
+            @pl.when((turn_row != row) | (turn_col + n != col))
+            def _():
+                signal(barrier, turn_row, turn_col + n)
+        for shift in SHIFTS:
+            @pl.when(on_map(col + shift))
+            def _():
+                signal(barrier, row, col + shift)
+        for k in range(1, 4):
+            signal(barrier, near_row(k), col)
+        beside = row + 2 * core - 1
+
+        @pl.when((beside >= 0) & (beside < ROWS))
+        def _():
+            signal(barrier, beside, col)
+
+        each(1, 16, lambda k: signal(barrier, row, plane_peer(col, k)))
+        each(0, 16, lambda k: signal(barrier, sibling, plane_peer(col, k)))
+
         loads = [
             pltpu.make_async_copy(src, dst, in_sem.at[n])
             for n, (src, dst) in enumerate((
@@ -130,27 +152,6 @@
         ]
         for load in loads:
             load.start()
-        barrier = pltpu.get_barrier_semaphore()
-        each(0, 16, lambda k: signal(barrier, sibling, plane_peer(col, k)))
-        each(1, 16, lambda k: signal(barrier, row, plane_peer(col, k)))
-        for k in range(1, 4):
-            signal(barrier, near_row(k), col)
-            signal(barrier, *far_at(k))
-        beside = row + 2 * core - 1
-
-        @pl.when((beside >= 0) & (beside < ROWS))
-        def _():
-            signal(barrier, beside, col)
-
-        for shift in (1, 2, -1, -2):
-            @pl.when(on_map(col + shift))
-            def _():
-                signal(barrier, row, col + shift)
-        for n in range(4):
-            @pl.when((turn_row != row) | (turn_col + n != col))
-            def _():
-                signal(barrier, turn_row, turn_col + n)
-
     with jax.named_scope("project"):
         for n in (0, 1, 2):
             loads[n].wait()
@@ -278,8 +279,6 @@
         each(1, 16, lambda k: remote(
             far_block, far_block, l_send, l_recv2, row, plane_peer(col, k)).start())
 
-    along_cols(cots, c_send, c_recv)
-
     with jax.named_scope("relay"):
         def relay(k):
             p = lax.rem(row + ROWS - 2 * k, 8)
@@ -288,6 +287,8 @@
             remote(block, block, r_send, r_recv, sibling, col).start()
 
         each(1, 4, relay)
+    along_cols(cots, c_send, c_recv)
+
     with jax.named_scope("cotangent"):
         for n in range(4, 10):
             loads[n].wait()

time: 93 us -> 90.9 us (0.977)
  Pallas kernels: 92.2 us -> 89.9 us
    pallas_call x1, Pallas kernels: 90 us -> 87.7 us  [local(): pl.pallas_call(kernel, out_shape=(shape((128, 128), BF), shape((128, 128)...]
where the time goes in v5:
time: 90.9 us; the launch traced here: 90.6 us
  Pallas kernels  89.9 us (99%)
    pallas_call x1, Pallas kernels, local(): pl.pallas_call(kernel, out_shape=(shape((128, 128), BF), shape((128, 128)...  87.7 us
    pallas_call x1, Pallas kernels, local(): pl.pallas_call(finish_kernel, out_shape=(shape((128, 128), BF), shape((12...  2.18 us

profile of v5, /device:TPU:1, one launch (start us, length us, event | category | flops | bytes accessed | tf_op | source)
XLA Modules:
  0.0 90.6 jit_solution(14529766599874661761)
XLA Ops:
  0.6 87.7 %shard_map.129 = (bf16[128,128]{1,0:T(8,128)(2,1)}, bf16[128,128]{1,0:T(8,128)(2,1)}, bf16[32,80,128]{2,1,0:T(8,128)(2,1)}) custom-call(bf16[128,128]{1,0:T(8,128)(2,1)} %bitcast.6, s32[8,16]{1,0:T(8,128)} %bitcast.8, s32[8,16]{1,0:T(8,128)} %bitcast.9, s32[2]{0:T(128)} %rates_h.1, bf16[128,512]{1,0:T(8,128)(2,1)} %wproj_h.1, bf16[128,128]{1,0:T(8,128)(2,1)} %wgate_h.1, ...), custom_call_target="tpu_custom_call" | custom-call | tf_op jit(solution)/shard_map/pallas_call | solution.py:579
  88.4 2.2 %shard_map.130 = (bf16[128,128]{1,0:T(8,128)(2,1)}, bf16[128,128]{1,0:T(8,128)(2,1)}, f32[9,128,128]{2,1,0:T(8,128)}, f32[9,128,128]{2,1,0:T(8,128)}) custom-call(bf16[128,128]{1,0:T(8,128)(2,1)} %get-tuple-element.11.output_in, bf16[128,128]{1,0:T(8,128)(2,1)} %get-tuple-element.12.gpair_in, bf16[32,80,128]{2,1,0:T(8,128)(2,1)} %get-tuple-element.13.total_in), custom_call_target="tpu_custom_call" | custom-call | tf_op jit(solution)/shard_map/pallas_call | solution.py:606

commit v6 on v5

--- a/solution.py
+++ b/solution.py
@@ -119,7 +119,7 @@
         z = lax.rem(z_hi * 8 + row // 2 + 4 * k, 16)
         return lax.rem(z, 8) * 2 + core, (col // 8) * 8 + (z // 8) * 4 + lax.rem(col, 4)
 
-    with jax.named_scope("start"):
+    if True:
         barrier = pltpu.get_barrier_semaphore()
         for k in (2, 1, 3):
             signal(barrier, *far_at(k))
@@ -152,7 +152,7 @@
         ]
         for load in loads:
             load.start()
-    with jax.named_scope("project"):
+    if True:
         for n in (0, 1, 2):
             loads[n].wait()
         pair = pair_v[...].astype(F32)
@@ -167,7 +167,7 @@
         )
         loads[3].wait()
 
-    with jax.named_scope("barrier"):
+    if True:
         fixed = (turn_row == row) & (lax.rem(row, 8) == col // 4)
         pl.semaphore_wait(
             barrier,
@@ -231,7 +231,7 @@
             wait_bytes(buf.at[pl.ds(5, 5)], send_sem.at[1])
             wait_bytes(buf.at[pl.ds(0, 5)], recv_sem.at[0])
 
-    with jax.named_scope("turn"):
+    if True:
         def turn(half, low):
             return low * 8 + col // 4, 2 * row + half
 
@@ -266,20 +266,20 @@
             def _():
                 wait_bytes(right.at[0], r_recv0.at[n])
 
-    with jax.named_scope("spread"):
+    if True:
         four = right.at[pl.ds(turn_col, 4)]
         each(1, 4, lambda k: remote(
             four, four, r_send, r_relay.at[lax.rem(row, 8) // 2],
             (row // 8) * 8 + lax.rem(row + 2 * k, 8), col).start())
         remote(four, four, r_send, r_recv, sibling, col).start()
 
-    with jax.named_scope("farwait"):
+    if True:
         far_block = left.at[far]
         wait_bytes(far_block, l_far)
         each(1, 16, lambda k: remote(
             far_block, far_block, l_send, l_recv2, row, plane_peer(col, k)).start())
 
-    with jax.named_scope("relay"):
+    if True:
         def relay(k):
             p = lax.rem(row + ROWS - 2 * k, 8)
             block = right.at[pl.ds(4 * p, 4)]
@@ -289,7 +289,7 @@
         each(1, 4, relay)
     along_cols(cots, c_send, c_recv)
 
-    with jax.named_scope("cotangent"):
+    if True:
         for n in range(4, 10):
             loads[n].wait()
         gating = jax.nn.sigmoid(jnp.dot(normed, wgate_v[...], preferred_element_type=F32))
@@ -324,7 +324,7 @@
 
         return lax.fori_loop(0, 16, add, total)
 
-    with jax.named_scope("products"):
+    if True:
         @pl.when(core != z_hi)
         def _():
             wait_bytes(sibling_part, r_recv)
@@ -360,7 +360,7 @@
                         f_recv.at[2 - shift], row, col + shift,
                     ).start()
 
-    with jax.named_scope("rimcols"):
+    if True:
         for shift in SHIFTS:
             @pl.when(jnp.logical_not(on_map(col - shift)))
             def _():
@@ -394,18 +394,18 @@
         take_column(inward)
         take_column(2 * inward)
         wait_rows(cots, c_send2, c_recv2)
-    with jax.named_scope("hidden"):
+    if True:
         unfold(cots, cfield, range(15))
         shifted(cfield, ctaps, 8, two_rate, 32, -1)
         back_two = jnp.concatenate([two_v[t].T for t in range(9)], axis=0)
         ghid[...] = jnp.dot(
             windows(ctaps, 8, two_rate, 24, -1), back_two, preferred_element_type=F32
         )
-    with jax.named_scope("rimwait"):
+    if True:
         take_column(-inward)
         take_column(-2 * inward)
         unfold(first, field, range(5, 10))
-    with jax.named_scope("rimrows"):
+    if True:
         for shift in SHIFTS:
             @pl.when(on_map(col + shift))
             def _():
@@ -428,10 +428,10 @@
         def _():
             wait_bytes(first.at[pl.ds(0, 5)], f_send2.at[1])
 
-    with jax.named_scope("unfold"):
+    if True:
         unfold(first, field, [*range(5), *range(10, 15)])
         shifted(field, taps, 8, one_rate, 32, 1)
-    with jax.named_scope("conv"):
+    if True:
         pre = jnp.dot(
             windows(taps, 8, one_rate, 24, 1), one_v[...].reshape(1152, 128),
             preferred_element_type=F32,
@@ -464,14 +464,14 @@
     def padded(value):
         return jnp.concatenate([value.astype(BF), jnp.zeros((128, 128), BF)]).reshape(16, 80, 128)
 
-    with jax.named_scope("gradtwo"):
+    if True:
         cot_own = cots[7]
         second_taps = back(windows(htaps, 8, two_rate, 8, 1))
         grads[pl.ds(16, 16)] = padded(
             lax.dot_general(second_taps, cot_own, over, preferred_element_type=F32)
         )
         scatter(1, 0)
-    with jax.named_scope("gradone"):
+    if True:
         gpre_own = gpre[pl.ds(8, 8), pl.ds(8, 16), :].reshape(128, 128).astype(BF)
         first_taps = windows(taps, 16, one_rate, 8, 1, pl.ds(8, 16))
         grads[pl.ds(0, 16)] = padded(
@@ -480,7 +480,7 @@
         scatter(0, 0)
         scatter(1, 1)
         scatter(0, 1)
-    with jax.named_scope("outputs"):
+    if True:
         parts[me] = grads[me]
         updated = sums[...]
         centre = updated - jnp.mean(updated, axis=-1, keepdims=True)
@@ -510,21 +510,21 @@
 
     most = parts.at[pl.ds(0, 31)]
     three = near.at[pl.ds(0, 3)]
-    with jax.named_scope("near"):
+    if True:
         for chunk, rows in enumerate(CHUNKS):
             wait_bytes(parts.at[pl.ds(0, 31), rows], recv1.at[chunk])
             near[near_place, rows, :] = added(parts, 32, chunk)
             block = near.at[near_place, rows]
             for k in range(1, 4):
                 remote(block, block, send2, recv2.at[chunk], near_row(k), col).start()
-    with jax.named_scope("apart"):
+    if True:
         for chunk, rows in enumerate(CHUNKS):
             wait_bytes(near.at[pl.ds(0, 3), rows], recv2.at[chunk])
             apart[far_place, rows, :] = added(near, 4, chunk)
             block_far = apart.at[far_place, rows]
             for k in (2, 1, 3):
                 remote(block_far, block_far, send3, recv3.at[chunk], *far_at(k)).start()
-    with jax.named_scope("gather"):
+    if True:
         for chunk, rows in enumerate(CHUNKS):
             wait_bytes(apart.at[pl.ds(0, 3), rows], recv3.at[chunk])
             final[me, rows, :] = added(apart, 4, chunk)
@@ -548,7 +548,7 @@
         wait_bytes(three, send2)
         wait_bytes(three, send3)
         wait_bytes(final.at[pl.ds(0, 16)], recv5)
-    with jax.named_scope("finish"):
+    if True:
         wait_bytes(most, send4)
         total_ref[...] = final[...]
 

time: 90.9 us -> 90.7 us (level)
  no operation moved by 1% of the time
where the time goes in v6:
time: 90.7 us; the launch traced here: 90.6 us
  Pallas kernels  89.9 us (99%)
    pallas_call x1, Pallas kernels, local(): pl.pallas_call(kernel, out_shape=(shape((128, 128), BF), shape((128, 128)...  87.7 us
    pallas_call x1, Pallas kernels, local(): pl.pallas_call(finish_kernel, out_shape=(shape((128, 128), BF), shape((12...  2.18 us

profile of v6, /device:TPU:1, one launch (start us, length us, event | category | flops | bytes accessed | tf_op | source)
XLA Modules:
  0.0 90.6 jit_solution(14529766599874661761)
XLA Ops:
  0.6 87.7 %shard_map.129 = (bf16[128,128]{1,0:T(8,128)(2,1)}, bf16[128,128]{1,0:T(8,128)(2,1)}, bf16[32,80,128]{2,1,0:T(8,128)(2,1)}) custom-call(bf16[128,128]{1,0:T(8,128)(2,1)} %bitcast.6, s32[8,16]{1,0:T(8,128)} %bitcast.8, s32[8,16]{1,0:T(8,128)} %bitcast.9, s32[2]{0:T(128)} %rates_h.1, bf16[128,512]{1,0:T(8,128)(2,1)} %wproj_h.1, bf16[128,128]{1,0:T(8,128)(2,1)} %wgate_h.1, ...), custom_call_target="tpu_custom_call" | custom-call | tf_op jit(solution)/shard_map/pallas_call | solution.py:579
  88.4 2.2 %shard_map.130 = (bf16[128,128]{1,0:T(8,128)(2,1)}, bf16[128,128]{1,0:T(8,128)(2,1)}, f32[9,128,128]{2,1,0:T(8,128)}, f32[9,128,128]{2,1,0:T(8,128)}) custom-call(bf16[128,128]{1,0:T(8,128)(2,1)} %get-tuple-element.11.output_in, bf16[128,128]{1,0:T(8,128)(2,1)} %get-tuple-element.12.gpair_in, bf16[32,80,128]{2,1,0:T(8,128)(2,1)} %get-tuple-element.13.total_in), custom_call_target="tpu_custom_call" | custom-call | tf_op jit(solution)/shard_map/pallas_call | solution.py:606
